TPU v7x, 128 devices: a whole 4x4x4 slice. The times are simulated.
128 devices in a mesh: row: 4 (over z), col: 8 (over y, core), slide: 4 (over x).
Axes of the slice: x: 4, y: 4, z: 4, core: 2. Of those that a mesh axis runs over, the one named last changes fastest.
Arguments:
- image: bfloat16 [4, 384, 768, 256], P('slide', 'row', 'col'), may hold values from -48 to 48
- reduce_weight: bfloat16 [256, 128], replicated, may hold values from -0.375 to 0.375
- spatial_weight: bfloat16 [3, 3, 128, 128], replicated, may hold values from -0.1875 to 0.1875
- expand_weight: bfloat16 [128, 512], replicated, may hold values from -0.5 to 0.5
- project_weight: bfloat16 [256, 512], replicated, may hold values from -0.375 to 0.375
- classify_weight: float32 [512, 2], replicated, may hold values from -0.6 to 0.6
- tissue_mask: int32 [4, 12, 24], P('slide'), may hold values from 0 to 1, as said below
- slide_labels: int32 [4], P('slide'), may hold values from 0 to 1
Outputs:
- grad_image: bfloat16 [4, 384, 768, 256], P('slide', 'row', 'col')
- grad_reduce: float32 [256, 128], replicated
- grad_spatial: float32 [3, 3, 128, 128], replicated
- grad_expand: float32 [128, 512], replicated
- grad_project: float32 [256, 512], replicated
- grad_classify: float32 [512, 2], replicated
- loss: float32 [], replicated
Inputs may be any that keep to these rules, and one draw needn't show every extreme that they name: `tissue_mask`: 1 marks a tissue tile and 0 background; every slide has at least one tissue tile.
All inputs are finite; a program needn't handle non-finite values.
Results may differ from a plain program's by a relative error of at most 0.0095.
Values may be sent and summed in bfloat16 or wider, within the bound.
A program may use at most 128 MiB of HBM per device.

v0:
```python
import jax
import jax.numpy as jnp
from jax import lax
from jax.sharding import PartitionSpec as P

BLK = 32


EPSILON = 1e-05


def shifted(value, axis, by):
    peers = lax.axis_size(axis)
    pairs = [(i, i + by) for i in range(peers) if 0 <= i + by < peers]
    return lax.ppermute(value, axis, pairs)


def normed(values):
    return values * lax.rsqrt(jnp.mean(values * values, axis=-1, keepdims=True) + EPSILON)


def activate(values):
    return jax.nn.silu(normed(values))


def gather_taps(padded, out_rows, out_cols):
    channels = padded.shape[-1]
    grid_view = padded.reshape(out_rows + 1, 2, out_cols + 1, 2, channels)
    pieces = []
    for row_tap in range(3):
        for col_tap in range(3):
            pieces.append(
                grid_view[
                    row_tap // 2 : row_tap // 2 + out_rows,
                    row_tap % 2,
                    col_tap // 2 : col_tap // 2 + out_cols,
                    col_tap % 2,
                ]
            )
    return jnp.concatenate(pieces, axis=-1)


def spread_taps(grads, spatial_flat):
    grad_rows, grad_cols, channels = grads.shape
    tap_terms = jnp.einsum("ijd,kd->ijk", grads, spatial_flat, preferred_element_type=jnp.float32)
    tap_terms = tap_terms.reshape(grad_rows, grad_cols, 3, 3, channels)
    parity_sums = [[None, None], [None, None]]
    for row_tap in range(3):
        for col_tap in range(3):
            placed = jnp.pad(
                tap_terms[:, :, row_tap, col_tap],
                ((row_tap // 2, 1 - row_tap // 2), (col_tap // 2, 1 - col_tap // 2), (0, 0)),
            )
            if parity_sums[row_tap % 2][col_tap % 2] is None:
                parity_sums[row_tap % 2][col_tap % 2] = placed
            else:
                parity_sums[row_tap % 2][col_tap % 2] = (
                    parity_sums[row_tap % 2][col_tap % 2] + placed
                )
    upper_half = jnp.stack([parity_sums[0][0], parity_sums[0][1]], axis=2)
    lower_half = jnp.stack([parity_sums[1][0], parity_sums[1][1]], axis=2)
    assembled = jnp.stack([upper_half, lower_half], axis=1)
    return assembled.reshape(2 * grad_rows + 2, 2 * grad_cols + 2, channels)


def per_device(
    image,
    reduce_weight,
    spatial_weight,
    expand_weight,
    project_weight,
    classify_weight,
    tissue_mask,
    slide_labels,
):
    pixels = image[0]
    pixel_rows, pixel_cols, in_channels = pixels.shape
    mid_channels = reduce_weight.shape[1]
    out_channels = expand_weight.shape[1]
    half_rows = pixel_rows // 2
    half_cols = pixel_cols // 2
    tile_side = BLK // 2
    block_rows = pixel_rows // BLK
    block_cols = pixel_cols // BLK
    tile_scale = float(tissue_mask.shape[1] * tissue_mask.shape[2])
    highest = lax.Precision.HIGHEST
    spatial_flat = spatial_weight.reshape(9 * mid_channels, mid_channels)
    pre_reduce = jnp.dot(pixels, reduce_weight, preferred_element_type=jnp.float32)
    reduced = activate(pre_reduce).astype(jnp.bfloat16)
    above_row = shifted(reduced[-1:], "row", 1)
    with_above = jnp.concatenate([above_row, reduced], axis=0)
    left_column = shifted(with_above[:, -1:], "col", 1)
    extended = jnp.concatenate([left_column, with_above], axis=1)
    padded = jnp.pad(extended, ((0, 1), (0, 1), (0, 0)))
    patches = gather_taps(padded, half_rows, half_cols)
    pre_spatial = jnp.dot(patches, spatial_flat, preferred_element_type=jnp.float32)
    spatial = activate(pre_spatial).astype(jnp.bfloat16)
    even_pixels = pixels.reshape(half_rows, 2, half_cols, 2, in_channels)[:, 0, :, 0]
    pre_expand = jnp.dot(spatial, expand_weight, preferred_element_type=jnp.float32)
    pre_project = jnp.dot(even_pixels, project_weight, preferred_element_type=jnp.float32)
    combined = normed(pre_expand) + normed(pre_project)
    merged = jax.nn.silu(combined)
    features = merged.reshape(block_rows, tile_side, block_cols, tile_side, out_channels).mean(
        axis=(1, 3)
    )
    logits = jnp.einsum("uvc,ck->uvk", features, classify_weight, precision=highest)
    label_sign = 1.0 - 2.0 * slide_labels[0].astype(jnp.float32)
    margin = (logits[..., 1] - logits[..., 0]) * label_sign
    whole_mask = tissue_mask[0]
    tissue = lax.dynamic_slice(
        whole_mask,
        (lax.axis_index("row") * block_rows, lax.axis_index("col") * block_cols),
        (block_rows, block_cols),
    ).astype(jnp.float32)
    tissue_tiles = jnp.sum(whole_mask.astype(jnp.float32))
    loss_local = jnp.sum(tissue * jnp.logaddexp(0.0, margin)) / tissue_tiles
    tile_weight = tissue * jax.nn.sigmoid(margin) / tissue_tiles
    logit_grad = jnp.stack([-tile_weight * label_sign, tile_weight * label_sign], axis=-1)
    grad_classify = jnp.einsum("uvc,uvk->ck", features, logit_grad, precision=highest)
    feature_grad = (
        jnp.einsum("uvk,ck->uvc", logit_grad, classify_weight, precision=highest) * tile_scale
    )
    spread_grad = jnp.broadcast_to(
        feature_grad[:, None, :, None, :],
        (block_rows, tile_side, block_cols, tile_side, out_channels),
    ).reshape(half_rows, half_cols, out_channels)
    merged_grad = jax.vjp(jax.nn.silu, combined)[1](spread_grad)[0]
    expand_grad = jax.vjp(normed, pre_expand)[1](merged_grad)[0].astype(jnp.bfloat16)
    project_grad = jax.vjp(normed, pre_project)[1](merged_grad)[0].astype(jnp.bfloat16)
    grad_expand = jnp.einsum(
        "ijc,ijd->cd", spatial, expand_grad, preferred_element_type=jnp.float32
    )
    grad_project = jnp.einsum(
        "ijc,ijd->cd", even_pixels, project_grad, preferred_element_type=jnp.float32
    )
    spatial_grad = jnp.einsum(
        "ijd,cd->ijc", expand_grad, expand_weight, preferred_element_type=jnp.float32
    )
    pre_spatial_grad = jax.vjp(activate, pre_spatial)[1](spatial_grad)[0].astype(jnp.bfloat16)
    grad_spatial = jnp.einsum(
        "ijk,ijd->kd", patches, pre_spatial_grad, preferred_element_type=jnp.float32
    )
    spread = spread_taps(pre_spatial_grad, spatial_flat)[: pixel_rows + 1, : pixel_cols + 1]
    right_part = shifted(spread[:, :1], "col", -1)
    spread = jnp.concatenate([spread[:, 1:-1], spread[:, -1:] + right_part], axis=1)
    lower_part = shifted(spread[:1], "row", -1)
    reduced_grad = jnp.concatenate([spread[1:-1], spread[-1:] + lower_part], axis=0)
    pre_reduce_grad = jax.vjp(activate, pre_reduce)[1](reduced_grad)[0].astype(jnp.bfloat16)
    grad_reduce = jnp.einsum(
        "hwc,hwd->cd", pixels, pre_reduce_grad, preferred_element_type=jnp.float32
    )
    main_grad = jnp.einsum(
        "hwd,cd->hwc", pre_reduce_grad, reduce_weight, preferred_element_type=jnp.float32
    )
    side_grad = jnp.einsum(
        "ijd,cd->ijc", project_grad, project_weight, preferred_element_type=jnp.float32
    )
    side_full = jnp.pad(
        side_grad[:, None, :, None, :], ((0, 0), (0, 1), (0, 0), (0, 1), (0, 0))
    ).reshape(pixel_rows, pixel_cols, in_channels)
    grad_image = (main_grad + side_full).astype(jnp.bfloat16)[None]
    sum_reduce, sum_spatial, sum_expand, sum_project, sum_classify, loss_total = lax.psum(
        (grad_reduce, grad_spatial, grad_expand, grad_project, grad_classify, loss_local),
        ("row", "col", "slide"),
    )
    return (
        grad_image,
        sum_reduce / tile_scale,
        sum_spatial.reshape(3, 3, mid_channels, mid_channels) / tile_scale,
        sum_expand / tile_scale,
        sum_project / tile_scale,
        sum_classify,
        loss_total,
    )


def solution(mesh):
    in_specs = (
        P("slide", "row", "col", None),
        P(),
        P(),
        P(),
        P(),
        P(),
        P("slide", None, None),
        P("slide"),
    )
    out_specs = (P("slide", "row", "col", None), P(), P(), P(), P(), P(), P())
    return jax.shard_map(
        per_device, mesh=mesh, in_specs=in_specs, out_specs=out_specs, check_vma=False
    )
```

profile of v0, /device:TPU:1, one launch (start us, length us, event | category | flops | bytes accessed | tf_op | source)
XLA Modules:
  0.0 298.9 jit_solution(12584770986070654677)
XLA Ops:
  7.2 4.3 %multiply_reduce_fusion.5 = (f32[96,96]{1,0:T(8,128)S(1)}, f32[96,96,128]{2,1,0:T(8,128)S(1)}) fusion(bf16[256,128]{1,0:T(8,128)(2,1)} %param.9, bf16[1,96,96,256]{3,2,1,0:T(8,128)(2,1)} %param.8), kind=kOutput, calls=%fused_computation.38 | convolution fusion | flops 606329856 | bytes 9539584 | tf_op jit(solution)/shard_map/dot_general | solution.py:88
  13.7 4.4 %collective-permute-start = (bf16[1,96,128]{2,1,0:T(8,128)(2,1)S(1)}, bf16[1,96,128]{2,1,0:T(8,128)(2,1)S(1)}, u32[]{:S(2)}, u32[]{:S(2)}) collective-permute-start(bf16[1,96,128]{2,1,0:T(8,128)(2,1)S(1)} %slice.120), channel_id=1, source_target_pairs={{0,32},{32,64},{64,96},{1,33},{33,65},{65,97},{2,34},{34,66},{66,9... | collective-permute-start | bytes 73736 | tf_op jit(solution)/shard_map/ppermute | solution.py:15
  18.1 8.0 %reshape_squeeze.3 = bf16[48,2,48,2,256]{4,3,2,1,0:T(2,128)(2,1)} reshape(bf16[1,96,96,256]{3,2,1,0:T(8,128)(2,1)} %param.8) | data formatting | bytes 9437184 | tf_op jit(solution)/shard_map/reshape;squeeze | solution.py:98
  26.1 3.7 %slice.130 = bf16[48,1,48,1,256]{4,3,2,1,0:T(2,128)(2,1)S(1)} slice(bf16[48,2,48,2,256]{4,3,2,1,0:T(2,128)(2,1)} %reshape_squeeze.3), slice={[0:48], [0:1], [0:48], [0:1], [0:256]} | slice | bytes 2359296 | tf_op jit(solution)/shard_map/slice | solution.py:98
  29.9 2.9 multiply_reduce_fusion.3
  32.8 4.6 %collective-permute-start.1 = (bf16[97,1,128]{2,1,0:T(2,128)(2,1)S(1)}, bf16[97,1,128]{2,1,0:T(2,128)(2,1)S(1)}, u32[]{:S(2)}, u32[]{:S(2)}) collective-permute-start(bf16[97,1,128]{2,1,0:T(2,128)(2,1)S(1)} %pad_maximum_fusion.2), channel_id=1, source_target_pairs={{0,4},{4,8},{8,12},{12,16},{16,20},{20,24},{24,28},{1,5},{5,9},{9,... | collective-permute-start | bytes 74504 | tf_op jit(solution)/shard_map/ppermute | solution.py:15
  38.7 4.0 %fusion.21 = bf16[98,98,128]{2,1,0:T(8,128)(2,1)} fusion(bf16[97,1,128]{2,1,0:T(2,128)(2,1)S(1)} %collective-permute-done.1, bf16[96,96,128]{2,1,0:T(8,128)(2,1)S(1)} %multiply_convert_fusion, bf16[1,96,128]{2,1,0:T(8,128)(2,1)S(1)} %collective-permute-done), kind=kLoop, calls=%fused_computation.46 | loop fusion | flops 18439680 | bytes 4867328 | tf_op jit(solution)/shard_map/concatenate | solution.py:93
  42.7 5.1 %reshape.126 = bf16[49,2,49,2,128]{4,3,2,1,0:T(2,128)(2,1)S(1)} reshape(bf16[98,98,128]{2,1,0:T(8,128)(2,1)} %fusion.21) | data formatting | bytes 4917248 | tf_op jit(solution)/shard_map/reshape | solution.py:28
  47.7 8.6 %fusion.74 = (bf16[48,1,48,1,128]{4,3,2,1,0:T(2,128)(2,1)S(1)}, bf16[48,1,48,1,128]{4,3,2,1,0:T(2,128)(2,1)S(1)}, bf16[48,1,48,1,128]{4,3,2,1,0:T(2,128)(2,1)S(1...) fusion(bf16[49,2,49,2,128]{4,3,2,1,0:T(2,128)(2,1)S(1)} %reshap, ...), kind=kLoop, calls=%fused_computation.154 | loop fusion | bytes 10616832 | tf_op jit(solution)/shard_map/slice | solution.py:33
  62.9 2.9 fusion.16
  71.0 5.7 %multiply_reduce_fusion.2 = (f32[48,48]{1,0:T(8,128)S(1)}, f32[48,48]{1,0:T(8,128)S(1)}, f32[48,48,512]{2,1,0:T(8,128)S(1)}) fusion(f32[48,48,512]{2,1,0:T(8,128)S(1)} %copy-done.4, f32[48,48,512]{2,1,0:T(8,128)} %get-tuple-element.59, f32[48,48,512]{2,1,0:T(8,128)S(1)} %bitcast.202, f32[48,48]{1,0:T(8,128)S(1)} %get-tuple-element.65, ...), kind=kLoop, calls=%fused_computation.30 | loop fusion | flops 18869760 | bytes 18911232 | tf_op jit(solution)/shard_map/transpose(jvp())/reduce_sum | solution.py:19
  86.6 4.1 %slice_bitcast_fusion.8 = (f32[48,48,128]{2,1,0:T(8,128)}, f32[48,48,128]{2,1,0:T(8,128)}, f32[48,48,128]{2,1,0:T(8,128)}, f32[48,48,128]{2,1,0:T(8,128)}, f32[4...) fusion(f32[48,48,3,3,128]{4,1,3,2,0:T(8,128)S(1)} %fusion.38), kind=kLoop, calls=%fused_computation.68 | loop fusion | bytes 21233664 | tf_op jit(solution)/shard_map/squeeze | solution.py:51
  97.2 4.7 %copy.54 = f32[49,2,49,2,128]{4,3,2,1,0:T(2,128)} copy(f32[49,2,49,2,128]{4,2,0,3,1:T(8,128)S(1)} %pad_maximum_fusion) | data formatting | bytes 9834496 | tf_op jit(solution)/shard_map/stack | solution.py:62
  101.8 7.3 %reshape.130 = f32[98,98,128]{2,1,0:T(8,128)} reshape(f32[49,2,49,2,128]{4,3,2,1,0:T(2,128)} %copy.54) | data formatting | bytes 9834496 | tf_op jit(solution)/shard_map/reshape | solution.py:63
  112.3 3.4 %convolution_bitcast_fusion.2 = f32[256,512]{0,1:T(8,128)} fusion(bf16[48,48,512]{2,1,0:T(8,128)(2,1)S(1)} %get-tuple-element.44, bf16[48,1,48,1,256]{4,3,2,1,0:T(2,128)(2,1)} %copy-done.7), kind=kOutput, calls=%fused_computation.56 | convolution fusion | flops 603979776 | bytes 4063232 | tf_op jit(solution)/shard_map/ijc,ijd->cd/dot_general | solution.py:133
  120.8 3.2 %collective-permute-done.3 = f32[1,96,128]{2,1,0:T(8,128)S(1)} collective-permute-done((f32[1,96,128]{2,1,0:T(8,128)S(1)}, f32[1,96,128]{2,1,0:T(8,128)S(1)}, u32[]{:S(2)}, u32[]{:S(2)}) %collective-permute-start.3) | collective-permute-done | bytes 49184 | tf_op jit(solution)/shard_map/ppermute | solution.py:15
  124.1 4.0 %multiply_reduce_fusion.1 = f32[96,96]{1,0:T(8,128)S(1)} fusion(f32[96,96,128]{2,1,0:T(8,128)S(1)} %bitcast.195, f32[96,96]{1,0:T(8,128)S(1)} %fusion.51, f32[1,96,128]{2,1,0:T(8,128)S(1)} %fusion.50, f32[95,96,128]{2,1,0:T(8,128)S(1)} %fusion.17), kind=kLoop, calls=%fused_computation.29 | loop fusion | flops 15326208 | bytes 9510912 | tf_op jit(solution)/shard_map/transpose(jvp())/reduce_sum | solution.py:19
  128.1 3.8 %fusion.9 = bf16[96,96,128]{2,1,0:T(8,128)(2,1)S(1)} fusion(f32[96,96,128]{2,1,0:T(8,128)S(1)} %bitcast.195, f32[96,96]{1,0:T(8,128)S(1)} %multiply_multiply_fusion, f32[96,96]{1,0:T(8,128)S(1)} %fusion.51, f32[1,96,128]{2,1,0:T(8,128)S(1)} %fusion.50, f32[95,96,128]{2,1,0:T(8,128)S(1)} %fusion.17), kind=kLoop, calls=%fused_computation.20 | loop fusion | flops 18874368 | bytes 11870208 | tf_op jit(solution)/shard_map/convert_element_type | solution.py:148
  135.6 5.6 %copy.79 = f32[48,1,48,1,256]{4,3,2,1,0:T(1,128)} copy(f32[48,1,48,1,256]{4,2,0,3,1:T(8,128)} %convolution_bitcast_fusion.1) | data formatting | bytes 4718592
  141.2 9.4 %pad.49.clone = f32[48,2,48,2,256]{4,3,2,1,0:T(2,128)} pad(f32[48,1,48,1,256]{4,3,2,1,0:T(1,128)} %copy.79, f32[]{:T(128)} %constant.68.clone.1), padding=0_0x0_1x0_0x0_1x0_0 | pad | bytes 11796484 | tf_op jit(solution)/shard_map/jit(_pad)/pad | solution.py:158
  150.6 12.4 %reshape.131 = f32[96,96,256]{2,1,0:T(8,128)} reshape(f32[48,2,48,2,256]{4,3,2,1,0:T(2,128)} %pad.49.clone) | data formatting | bytes 18874368 | tf_op jit(solution)/shard_map/reshape | solution.py:160
  163.2 67.2 %all-reduce.11 = (f32[512,2]{0,1:T(2,128)}, f32[]{:T(128)}) all-reduce(f32[512,2]{0,1:T(2,128)S(1)} %convolution_bitcast_fusion.4, f32[]{:T(128)S(6)} %div.147), channel_id=1, replica_groups=mesh['row'=4,'col'=8,'slide'=4] {'row','col','slide'}, use_global_device_ids=true, to_apply=%region_14.15 | all-reduce | flops 1025 | bytes 8200 | tf_op jit(solution)/shard_map/psum | solution.py:162
  230.4 7.3 %fusion.11 = bf16[1,96,96,256]{3,2,1,0:T(8,128)(2,1)} fusion(f32[96,96,256]{2,1,0:T(8,128)} %reshape.131, bf16[96,96,128]{2,1,0:T(8,128)(2,1)S(1)} %fusion.9, bf16[256,128]{1,0:T(8,128)(2,1)S(1)} %copy-done.18), kind=kOutput, calls=%fused_computation.22 | convolution fusion | flops 608698368 | bytes 16580608 | tf_op jit(solution)/shard_map/hwd,cd->hwc/dot_general | solution.py:152
  237.7 48.5 %all-reduce.15.cloned.1.call-done = (f32[256,128]{0,1:T(8,128)}, f32[1152,128]{1,0:T(8,128)}, f32[128,512]{1,0:T(8,128)}, f32[256,512]{0,1:T(8,128)}) async-done(((f32[256,128]{0,1:T(8,128)}, f32[1152,128]{1,0:T(8,128)}, f32[128,512]{1,0:T(8,128)}, f32[256,512]{0,1:T(8,128)}), (f32[256,128]{0,1:T(8,128)}, f32[1152,128]{1,0:T(8,128)}, f32[128,512]{1,0:T(8,128)}, ...) | async-done | bytes 1507344 | tf_op jit(solution)/shard_map/psum | solution.py:162
  (137 shorter events, 46.9 us)
Async XLA Ops:
  7.2 50.8 %copy-start = (bf16[3,3,128,128]{3,2,1,0:T(8,128)(2,1)S(1)}, bf16[3,3,128,128]{3,2,1,0:T(8,128)(2,1)}, u32[]{:S(2)}) copy-start(bf16[3,3,128,128]{3,2,1,0:T(8,128)(2,1)} %param.10) | copy-start | bytes 884740
  7.2 279.0 %all-reduce.15.cloned.1.call-start = ((), (), s32[]{:S(2)}) async-start(), calls=%async_computation | async-start | bytes 3014656 | tf_op jit(solution)/shard_map/psum | solution.py:162
  13.7 19.0 %collective-permute-start = (bf16[1,96,128]{2,1,0:T(8,128)(2,1)S(1)}, bf16[1,96,128]{2,1,0:T(8,128)(2,1)S(1)}, u32[]{:S(2)}, u32[]{:S(2)}) collective-permute-start(bf16[1,96,128]{2,1,0:T(8,128)(2,1)S(1)} %slice.120), channel_id=1, source_target_pairs={{0,32},{32,64},{64,96},{1,33},{33,65},{65,97},{2,34},{34,66},{66,9... | collective-permute-start | bytes 73736 | tf_op jit(solution)/shard_map/ppermute | solution.py:15
  26.1 3.7 %copy-start.17 = (bf16[256,512]{1,0:T(8,128)(2,1)S(1)}, bf16[256,512]{1,0:T(8,128)(2,1)}, u32[]{:S(2)}) copy-start(bf16[256,512]{1,0:T(8,128)(2,1)} %param.12) | copy-start | bytes 786436
  29.9 7.5 %copy-start.22 = (s32[1,12,24]{2,0,1:T(1,128)S(1)}, s32[1,12,24]{2,0,1:T(1,128)}, u32[]{:S(2)}) copy-start(s32[1,12,24]{2,0,1:T(1,128)} %param.14) | copy-start | bytes 3460
  32.8 5.9 %collective-permute-start.1 = (bf16[97,1,128]{2,1,0:T(2,128)(2,1)S(1)}, bf16[97,1,128]{2,1,0:T(2,128)(2,1)S(1)}, u32[]{:S(2)}, u32[]{:S(2)}) collective-permute-start(bf16[97,1,128]{2,1,0:T(2,128)(2,1)S(1)} %pad_maximum_fusion.2), channel_id=1, source_target_pairs={{0,4},{4,8},{8,12},{12,16},{16,20},{20,24},{24,28},{1,5},{5,9},{9,... | collective-permute-start | bytes 74504 | tf_op jit(solution)/shard_map/ppermute | solution.py:15
  58.0 4.6 %slice-start.2 = ((s8[4718592]{0:T(1024)(128)(4,1)}), s8[4194304]{0:T(1024)(128)(4,1)S(1)}, s32[]{:S(2)}) async-start(s8[4718592]{0:T(1024)(128)(4,1)} %bitcast.196), calls=%async_computation.3 | async-start | bytes 8388608
  61.7 4.1 %copy-start.3 = (f32[48,48,512]{2,1,0:T(8,128)}, f32[48,48,512]{2,1,0:T(8,128)S(1)}, u32[]{:S(2)}) copy-start(f32[48,48,512]{2,1,0:T(8,128)S(1)} %get-tuple-element.61) | copy-start | bytes 14155780
  70.8 6.0 %slice-start.4 = ((s8[4718592]{0:T(1024)(128)(4,1)}), s8[4194304]{0:T(1024)(128)(4,1)S(1)}, s32[]{:S(2)}) async-start(s8[4718592]{0:T(1024)(128)(4,1)} %bitcast.198), calls=%async_computation.5 | async-start | bytes 8388608
  71.0 5.8 %slice-start.5 = ((s8[4718592]{0:T(1024)(128)(4,1)}), s8[524288]{0:T(1024)(128)(4,1)S(1)}, s32[]{:S(2)}) async-start(s8[4718592]{0:T(1024)(128)(4,1)} %bitcast.198), calls=%async_computation.6 | async-start | bytes 1048576
  78.9 3.7 %slice-start.8 = ((s8[5308416]{0:T(1024)(128)(4,1)}), s8[4194304]{0:T(1024)(128)(4,1)S(1)}, s32[]{:S(2)}) async-start(s8[5308416]{0:T(1024)(128)(4,1)} %bitcast.204), calls=%async_computation.9 | async-start | bytes 8388608
  90.7 3.6 %copy-start.14 = (f32[48,48,128]{2,1,0:T(8,128)S(1)}, f32[48,48,128]{2,1,0:T(8,128)}, u32[]{:S(2)}) copy-start(f32[48,48,128]{2,1,0:T(8,128)} %get-tuple-element.39) | copy-start | bytes 3538948
  90.7 3.6 %copy-start.15 = (f32[48,48,128]{2,1,0:T(8,128)S(1)}, f32[48,48,128]{2,1,0:T(8,128)}, u32[]{:S(2)}) copy-start(f32[48,48,128]{2,1,0:T(8,128)} %get-tuple-element.40) | copy-start | bytes 3538948
  110.1 8.6 %collective-permute-start.2 = (f32[97,1,128]{2,1,0:T(1,128)S(1)}, f32[97,1,128]{2,1,0:T(1,128)S(1)}, u32[]{:S(2)}, u32[]{:S(2)}) collective-permute-start(f32[97,1,128]{2,1,0:T(1,128)S(1)} %slice.144), channel_id=1, source_target_pairs={{4,0},{8,4},{12,8},{16,12},{20,16},{24,20},{28,24},{5,1},{9,5},{13... | collective-permute-start | bytes 149000 | tf_op jit(solution)/shard_map/ppermute | solution.py:15
  112.3 5.7 %copy-start.5 = (f32[98,98,128]{2,1,0:T(8,128)S(1)}, f32[98,98,128]{2,1,0:T(8,128)}, u32[]{:S(2)}) copy-start(f32[98,98,128]{2,1,0:T(8,128)} %reshape.130) | copy-start | bytes 14751748
  118.8 5.3 %slice-start = ((s8[4718592]{0:T(1024)(128)(4,1)}), s8[4194304]{0:T(1024)(128)(4,1)S(1)}, s32[]{:S(2)}) async-start(s8[4718592]{0:T(1024)(128)(4,1)} %bitcast.194), calls=%async_computation.1 | async-start | bytes 8388608
  118.8 5.3 %slice-start.1 = ((s8[4718592]{0:T(1024)(128)(4,1)}), s8[524288]{0:T(1024)(128)(4,1)S(1)}, s32[]{:S(2)}) async-start(s8[4718592]{0:T(1024)(128)(4,1)} %bitcast.194), calls=%async_computation.2 | async-start | bytes 1048576
  118.8 5.2 %collective-permute-start.3 = (f32[1,96,128]{2,1,0:T(8,128)S(1)}, f32[1,96,128]{2,1,0:T(8,128)S(1)}, u32[]{:S(2)}, u32[]{:S(2)}) collective-permute-start(f32[1,96,128]{2,1,0:T(8,128)S(1)} %pad_maximum_fusion.3), channel_id=1, source_target_pairs={{32,0},{64,32},{96,64},{33,1},{65,33},{97,65},{34,2},{66,34},{98,6... | collective-permute-start | bytes 147464 | tf_op jit(solution)/shard_map/ppermute | solution.py:15
  124.1 7.8 %slice-start.6 = ((s8[4718592]{0:T(1024)(128)(4,1)}), s8[4194304]{0:T(1024)(128)(4,1)S(1)}, s32[]{:S(2)}) async-start(s8[4718592]{0:T(1024)(128)(4,1)} %bitcast.200), calls=%async_computation.7 | async-start | bytes 8388608
  128.1 3.8 %slice-start.7 = ((s8[4718592]{0:T(1024)(128)(4,1)}), s8[524288]{0:T(1024)(128)(4,1)S(1)}, s32[]{:S(2)}) async-start(s8[4718592]{0:T(1024)(128)(4,1)} %bitcast.200), calls=%async_computation.8 | async-start | bytes 1048576
  150.6 79.8 %copy-start.18 = (bf16[256,128]{1,0:T(8,128)(2,1)S(1)}, bf16[256,128]{1,0:T(8,128)(2,1)}, u32[]{:S(2)}) copy-start(bf16[256,128]{1,0:T(8,128)(2,1)} %param.9) | copy-start | bytes 196612
  230.4 61.3 %copy-start.1 = (bf16[3,3,128,128]{3,2,1,0:T(8,128)(2,1)S(1)}, bf16[3,3,128,128]{3,2,1,0:T(8,128)(2,1)}, u32[]{:S(2)}) copy-start(bf16[3,3,128,128]{3,2,1,0:T(8,128)(2,1)} %param.10) | copy-start | bytes 884740
  286.2 4.1 %copy-start.19 = (f32[128,512]{1,0:T(8,128)S(1)}, f32[128,512]{1,0:T(8,128)}, u32[]{:S(2)}) copy-start(f32[128,512]{1,0:T(8,128)} %get-tuple-element.27) | copy-start | bytes 786436
  286.2 4.8 %copy-start.20 = (f32[256,128]{0,1:T(8,128)S(1)}, f32[256,128]{0,1:T(8,128)}, u32[]{:S(2)}) copy-start(f32[256,128]{0,1:T(8,128)} %get-tuple-element.25) | copy-start | bytes 393220
  (15 other events, 34.5 us)
Sparse Core Ops, SparseCore 0:
  133.7 152.3 all-reduce.14
where the time goes:
time: 304 us; the launch traced here: 299 us
  local copies, waits for them, and re-layouts  80.5 us (26%)
  blocking collectives  67.2 us (22%)
  waiting for transfers between devices  51.7 us (17%)
  other arithmetic  37.7 us (12%)
  matrix products  32.1 us (11%)
  between operations  17 us (6%)
  starting transfers between devices  12.7 us (4%)
    psum x1, blocking collectives, per_device(): lax.psum((grad_reduce, grad_spatial, grad_expand, grad_project, grad_clas...  67.2 us
    psum x1, waiting for transfers between devices, per_device(): lax.psum((grad_reduce, grad_spatial, grad_expand, grad_project, grad_clas...  48.5 us
    unnamed x79, local copies, waits for them, and re-layouts  13.1 us
    ppermute x4, starting transfers between devices, shifted(): return lax.ppermute(value, axis, pairs)  12.6 us
    reshape x1, local copies, waits for them, and re-layouts, per_device(): side_full = jnp.pad(side_grad[:, None, :, None, :], ((0, 0), (0, 1), (0,...  12.4 us
    reduce_sum x2, other arithmetic, normed(): values * lax.rsqrt(jnp.mean(values * values, axis=-1, keepdims=True) + EP...  9.69 us
    pad x1, local copies, waits for them, and re-layouts, per_device(): jnp.pad(side_grad[:, None, :, None, :], ((0, 0), (0, 1), (0, 0), (0, 1),...  9.43 us
    slice x1, local copies, waits for them, and re-layouts, gather_taps(): grid_view[row_tap // 2:row_tap // 2 + out_rows, row_tap % 2, col_tap // 2...  8.63 us
  transfers between devices with their start and end apart: 5, of which 2 were waited for; matrix products, arithmetic and copies ran while one was open for 19% of the time, Pallas kernels for 0%

commit v1 on v0

v1 whole, which is shorter than its diff:
```python
import jax
import jax.numpy as jnp
from jax import lax
from jax.experimental import pallas as pl
from jax.experimental.pallas import tpu as pltpu
from jax.sharding import PartitionSpec as P

EPSILON = 1e-05
MESH = pl.DeviceIdType.MESH
F32 = jnp.float32
BF16 = jnp.bfloat16

NR, NC, NS = 4, 8, 4
H = 96
Q = 48
CI, CM, CO = 256, 128, 512
TB = 16
SCALE = 1.0 / 288.0
CHUNK = 384
PIECE = CHUNK // (NR * NS)
IMG_CHUNKS = 12


def dot(a, b):
    return lax.dot_general(a, b, (((1,), (0,)), ((), ())), preferred_element_type=F32)


def dot_nt(a, b):
    return lax.dot_general(a, b, (((1,), (1,)), ((), ())), preferred_element_type=F32)


def dot_tn(a, b):
    return lax.dot_general(a, b, (((0,), (0,)), ((), ())), preferred_element_type=F32)


def lane_mean(x, n):
    return jnp.sum(x, axis=-1, keepdims=True) * (1.0 / n)


def rms_scale(v, n):
    return lax.rsqrt(lane_mean(v * v, n) + EPSILON)


def act(v):
    half = v * (0.5 * rms_scale(v, CM))
    return half * jnp.tanh(half) + half


def silu_slope(half):
    t = jnp.tanh(half)
    return (0.5 + 0.5 * t) * (1.0 + half * (1.0 - t))


def act_vjp(v, g):
    r = rms_scale(v, CM)
    n = v * r
    dn = g * silu_slope(0.5 * n)
    return r * (dn - n * lane_mean(dn * n, CM))


def loop(n, body):
    def step(i, carry):
        body(i)
        return carry

    lax.fori_loop(0, n, step, 0)


def kernel(
    img_hbm, wr, ws, we, wp, wc, mask, label,
    gimg_hbm, o_reduce, o_spatial, o_expand, o_project, o_classify, o_loss,
    img, pre, actb, rc_odd, rc_even, evp, evb, colb, col16, hcol, hcor, hcolf, srow,
    psp, spat, ne, npj, rs, feat, gb, eg, pg, dbuf, dcat, wback, eo, natb, prg16,
    dright, dcor, drightf, drow, dcol, ob,
    a_ws, a_we, a_wp, a_wr, a_misc,
    s1, r1, a1, r2, a3, s3, r4, s5, r5, a5, r6, r7,
    sem_in, sem_out, sem_h, sem_g, sem1, sem2, sem3, sem4, sem5, sem6, sem7,
):
    row, col, sld = lax.axis_index("row"), lax.axis_index("col"), lax.axis_index("slide")
    grp = row * NS + sld
    has_up, has_down = row > 0, row < NR - 1
    has_left, has_right = col > 0, col < NC - 1

    rows_in = H // IMG_CHUNKS

    def image_copy(k):
        return pltpu.make_async_copy(
            img_hbm.at[0, pl.ds(k * rows_in, rows_in)], img.at[pl.ds(k * rows_in, rows_in)], sem_in.at[k]
        )

    loop(IMG_CHUNKS, lambda k: image_copy(k).start())

    def col_peer(d):
        return {"col": lax.rem(col + d, NC)}

    def grp_peer(d):
        q = lax.rem(grp + d, NR * NS)
        return {"row": q // NS, "slide": lax.rem(q, NS)}

    barrier = pltpu.get_barrier_semaphore()
    loop(NC - 1, lambda d: pl.semaphore_signal(barrier, inc=1, device_id=col_peer(d + 1), device_id_type=MESH))
    loop(NR * NS - 1, lambda d: pl.semaphore_signal(barrier, inc=1, device_id=grp_peer(d + 1), device_id_type=MESH))
    to_diag = has_down & has_right
    from_diag = has_up & has_left

    @pl.when(to_diag)
    def _():
        pl.semaphore_signal(barrier, inc=1, device_id={"row": row + 1, "col": col + 1}, device_id_type=MESH)

    @pl.when(from_diag)
    def _():
        pl.semaphore_signal(barrier, inc=1, device_id={"row": row - 1, "col": col - 1}, device_id_type=MESH)

    wback[...] = jnp.zeros_like(wback)

    def tap(a, b):
        return ws[a, b * CM : (b + 1) * CM, :]

    for slot, a in ((0, 1), (1, 2), (2, 0)):
        wback[slot, 0:CM, 0:CM] = tap(a, 1)
        wback[slot, CM : 2 * CM, 0:CM] = tap(a, 2)
        wback[slot, CM : 2 * CM, CM : 2 * CM] = tap(a, 0)
    actb[:, 0:8, :] = jnp.zeros_like(actb[:, 0:8, :])
    dbuf[:, Q : Q + 8, :] = jnp.zeros_like(dbuf[:, Q : Q + 8, :])
    a_ws[...] = jnp.zeros_like(a_ws)
    a_we[...] = jnp.zeros_like(a_we)
    a_wp[...] = jnp.zeros_like(a_wp)
    a_wr[...] = jnp.zeros_like(a_wr)
    a_misc[...] = jnp.zeros_like(a_misc)

    @pl.when(jnp.logical_not(has_up))
    def _():
        rc_odd[0] = jnp.zeros_like(rc_odd[0])

    @pl.when(jnp.logical_not(has_left))
    def _():
        hcol[...] = jnp.zeros_like(hcol)

    @pl.when(jnp.logical_not(from_diag))
    def _():
        hcor[...] = jnp.zeros_like(hcor)

    @pl.when(jnp.logical_not(has_down))
    def _():
        dcat[Q] = jnp.zeros_like(dcat[Q])

    @pl.when(jnp.logical_not(has_right))
    def _():
        dright[...] = jnp.zeros_like(dright)

    @pl.when(jnp.logical_not(to_diag))
    def _():
        dcor[...] = jnp.zeros_like(dcor)

    eye = (
        lax.broadcasted_iota(jnp.int32, (CM, CM), 0) == lax.broadcasted_iota(jnp.int32, (CM, CM), 1)
    )
    wdiff = wc[:, 1:2] - wc[:, 0:1]
    drow_w = jnp.concatenate(
        [
            jnp.sum(jnp.where(eye, wdiff[k * CM : (k + 1) * CM], 0.0), axis=0, keepdims=True)
            for k in range(CO // CM)
        ],
        axis=1,
    )
    sign = 1.0 - 2.0 * label[0].astype(F32)
    tissue_all = mask[...].astype(F32)
    tiles = jnp.sum(jnp.sum(tissue_all, axis=1, keepdims=True), axis=0, keepdims=True)
    mask_r = lax.broadcasted_iota(jnp.int32, mask.shape, 0)
    mask_c = lax.broadcasted_iota(jnp.int32, mask.shape, 1)

    def pass1(k):
        image_copy(k).wait()
        x = img[pl.ds(k * 8, 8)].reshape(8 * H, CI)
        v = dot(x, wr[...])
        pre[pl.ds(k * 8, 8)] = v.reshape(8, H, CM)
        actb[:, 8 : 8 + H, :] = act(v).reshape(8, H, CM)
        for r in range(8):
            rows, at = (rc_even, k * 4 + r // 2) if r % 2 == 0 else (rc_odd, k * 4 + r // 2 + 1)
            for b in range(3):
                rows[at, :, b * CM : (b + 1) * CM] = actb[r, pl.ds(7 + b, Q, stride=2), :].astype(BF16)
            colb[pl.ds(k * 8 + r, 1), :] = actb[r, 7 + H : 8 + H, :]

    loop(IMG_CHUNKS, pass1)

    col16[...] = colb[...].astype(BF16)
    srow[...] = rc_odd[Q]

    def remote(src, dst, send, recv, device):
        return pltpu.make_async_remote_copy(
            src_ref=src, dst_ref=dst, send_sem=send, recv_sem=recv, device_id=device, device_id_type=MESH
        )

    down = remote(srow, rc_odd.at[0], sem_h.at[0], sem_h.at[1], {"row": lax.rem(row + 1, NR)})
    right = remote(col16, hcol, sem_h.at[2], sem_h.at[3], {"col": lax.rem(col + 1, NC)})
    diag = remote(
        col16.at[pl.ds(H - 16, 16)], hcor, sem_h.at[4], sem_h.at[5],
        {"row": lax.rem(row + 1, NR), "col": lax.rem(col + 1, NC)},
    )
    n_diag = jnp.where(to_diag, 1, 0) + jnp.where(from_diag, 1, 0)
    pl.semaphore_wait(barrier, NC - 1 + NR * NS - 1 + n_diag)
    forward = ((down, has_down, has_up), (right, has_right, has_left), (diag, to_diag, from_diag))
    for copy, sends, _ in forward:
        pl.when(sends)(copy.start)

    def even_rows(m):
        x = img[2 * m].astype(F32)
        for half in range(2):
            evb[half] = x[:, half * CM : (half + 1) * CM]
        for half in range(2):
            evp[m, :, half * CM : (half + 1) * CM] = evb[half, pl.ds(0, Q, stride=2), :].astype(BF16)

    loop(Q, even_rows)

    for copy, sends, takes in forward:
        pl.when(takes)(copy.wait_recv)
        pl.when(sends)(copy.wait_send)

    hcolf[0:H] = hcol[...].astype(F32)
    hcolf[H : H + 16] = hcor[...].astype(F32)
    first = lax.broadcasted_iota(jnp.int32, (16, CM), 0) == 0

    def patch_left(rows, at, value):
        old = rows[at, 0:16, 0:CM].astype(F32)
        rows[at, 0:16, 0:CM] = jnp.where(first, value, old).astype(BF16)

    patch_left(rc_odd, 0, hcolf[H + 15 : H + 16, :])

    def patch_rows(m):
        patch_left(rc_even, m, hcolf[pl.ds(2 * m, 1), :])
        patch_left(rc_odd, m + 1, hcolf[pl.ds(2 * m + 1, 1), :])

    loop(Q, patch_rows)

    npx = TB * Q

    def tile_row(u):
        i0 = u * TB

        def taps(a, at, n):
            if a == 1:
                return rc_even[pl.ds(at, n)].reshape(n * Q, 3 * CM)
            return rc_odd[pl.ds(at + a // 2, n)].reshape(n * Q, 3 * CM)

        def convolve(b):
            at = i0 + b * 8
            v = sum(dot(taps(a, at, 8), ws[a]) for a in range(3))
            psp[pl.ds(b * 8 * Q, 8 * Q), :] = v
            spat[pl.ds(b * 8 * Q, 8 * Q), :] = act(v).astype(BF16)

        loop(2, convolve)
        ne[...] = dot(spat[...], we[...])
        npj[...] = dot(evp[pl.ds(i0, TB)].reshape(npx, CI), wp[...])
        feat[...] = jnp.zeros_like(feat)

        def merge(i):
            for v in range(3):
                at = pl.ds(i * Q + v * TB, TB)
                e, p = ne[at, :], npj[at, :]
                r_e, r_p = rms_scale(e, CO), rms_scale(p, CO)
                n_e, n_p = e * r_e, p * r_p
                ne[at, :], npj[at, :] = n_e, n_p
                rs[0, at, :], rs[1, at, :] = (jnp.broadcast_to(r, (TB, CM)) for r in (r_e, r_p))
                half = 0.5 * (n_e + n_p)
                merged = half * jnp.tanh(half) + half
                feat[v] += merged[0:8] + merged[8:16]

        loop(TB, merge)

        for v in range(3):
            f = jnp.sum(feat[v], axis=0, keepdims=True) * (1.0 / (TB * TB))
            margin = jnp.sum(f * drow_w, axis=1, keepdims=True) * sign
            here = (mask_r == row * 3 + u) & (mask_c == col * 3 + v)
            tissue = jnp.where(here, tissue_all, 0.0)
            tissue = jnp.sum(jnp.sum(tissue, axis=1, keepdims=True), axis=0, keepdims=True)
            soft = jnp.maximum(margin, 0.0) + jnp.log(1.0 + jnp.exp(-jnp.abs(margin)))
            weight = tissue * (0.5 + 0.5 * jnp.tanh(0.5 * margin)) / tiles * sign
            for k in range(CO // CM):
                a_misc[k : k + 1, :] += f[:, k * CM : (k + 1) * CM] * weight
            a_misc[4:5, :] += jnp.broadcast_to(tissue * soft / tiles, (1, CM))
            gb[v : v + 1, :] = drow_w * (weight * 288.0)

        def unmerge(i):
            for v in range(3):
                at = pl.ds(i * Q + v * TB, TB)
                n_e, n_p = ne[at, :], npj[at, :]
                dn = gb[v : v + 1, :] * silu_slope(0.5 * (n_e + n_p))
                out = pl.ds(i0 * Q + i * Q + v * TB, TB)
                eg[at, :] = (rs[0, at, 0:1] * (dn - n_e * lane_mean(dn * n_e, CO))).astype(BF16)
                pg[out, :] = (rs[1, at, 0:1] * (dn - n_p * lane_mean(dn * n_p, CO))).astype(BF16)

        loop(TB, unmerge)

        a_we[...] += dot_tn(spat[...], eg[...])
        a_wp[...] += dot_tn(evp[pl.ds(i0, TB)].reshape(npx, CI), pg[pl.ds(i0 * Q, npx), :])

        def unconvolve(b):
            at = pl.ds(b * 8 * Q, 8 * Q)
            g = dot_nt(eg[at, :], we[...])
            d = act_vjp(psp[at, :], g)
            dbuf[:, 0:Q, :] = d.reshape(8, Q, CM)
            d16 = d.astype(BF16)
            dcat[pl.ds(i0 + b * 8, 8), :, 0:CM] = d16.reshape(8, Q, CM)
            for r in range(8):
                dcat[i0 + b * 8 + r, :, CM : 2 * CM] = dbuf[r, 1 : Q + 1, :].astype(BF16)
                dcol[pl.ds(i0 + b * 8 + r, 1), :] = dbuf[r, 0:1, :]
            for a in range(3):
                a_ws[:, a * 3 * CM : (a + 1) * 3 * CM] += dot_tn(d16, taps(a, i0 + b * 8, 8))

        loop(2, unconvolve)

    loop(3, tile_row)

    drow[...] = dcat[0]
    col16[0:Q] = dcol[...].astype(BF16)
    up = remote(drow, dcat.at[Q], sem_g.at[0], sem_g.at[1], {"row": lax.rem(row + NR - 1, NR)})
    left = remote(col16.at[pl.ds(0, Q)], dright, sem_g.at[2], sem_g.at[3], {"col": lax.rem(col + NC - 1, NC)})
    gaid = remote(
        col16.at[pl.ds(0, 16)], dcor, sem_g.at[4], sem_g.at[5],
        {"row": lax.rem(row + NR - 1, NR), "col": lax.rem(col + NC - 1, NC)},
    )
    backward = ((up, has_up, has_down), (left, has_left, has_right), (gaid, from_diag, to_diag))
    for copy, sends, _ in backward:
        pl.when(sends)(copy.start)

    for t in range(9):
        s1[t * CM : (t + 1) * CM, :] = a_ws[:, t * CM : (t + 1) * CM].T.astype(BF16)
    for q in range(4):
        s1[1152 + q * 128 : 1152 + (q + 1) * 128, :] = a_we[:, q * CM : (q + 1) * CM].astype(BF16)
        s1[1664 + q * 256 : 1664 + (q + 1) * 256, :] = a_wp[:, q * CM : (q + 1) * CM].astype(BF16)
    s1[2688:3072, :] = jnp.zeros((384, CM), BF16)

    for copy, sends, takes in backward:
        pl.when(takes)(copy.wait_recv)
        pl.when(sends)(copy.wait_send)

    drightf[0:Q] = dright[...].astype(F32)
    drightf[Q : Q + 16] = dcor[...].astype(F32)
    last = lax.broadcasted_iota(jnp.int32, (16, CM), 0) == 15

    def patch_right(at, value):
        old = dcat[at, Q - 16 : Q, CM : 2 * CM].astype(F32)
        dcat[at, Q - 16 : Q, CM : 2 * CM] = jnp.where(last, value, old).astype(BF16)

    loop(Q, lambda m: patch_right(m, drightf[pl.ds(m, 1), :]))
    patch_right(Q, drightf[Q : Q + 1, :])

    def pass3(b):
        i0 = b * 8
        here = dcat[pl.ds(i0, 8)].reshape(8 * Q, 2 * CM)
        below = dcat[pl.ds(i0 + 1, 8)].reshape(8 * Q, 2 * CM)
        eo[0] = dot_nt(here, wback[0]).reshape(8, Q, 2 * CM)
        eo[1] = (dot_nt(here, wback[1]) + dot_nt(below, wback[2])).reshape(8, Q, 2 * CM)

        def one_row(i):
            for rp in range(2):
                at = 2 * (i0 + i) + rp
                for cp in range(2):
                    v = pre[at, pl.ds(cp, Q, stride=2), :]
                    natb[rp, pl.ds(cp, Q, stride=2), :] = act_vjp(v, eo[rp, i, :, cp * CM : (cp + 1) * CM])
                prg16[at] = natb[rp].astype(BF16)

        loop(8, one_row)
        rows = pl.ds(2 * i0, 16)
        a_wr[...] += dot_tn(prg16[rows].reshape(16 * H, CM), img[rows].reshape(16 * H, CI))

    loop(6, pass3)

    def image_out(k):
        rows = pl.ds(k * 8, 8)
        return pltpu.make_async_copy(img.at[rows], gimg_hbm.at[0, rows], sem_out.at[k])

    def pass4(k):
        main = dot_nt(prg16[pl.ds(k * 8, 8)].reshape(8 * H, CM), wr[...])
        side = dot_nt(pg[pl.ds(k * 4 * Q, 4 * Q), :], wp[...])
        for half in range(2):
            ob[half] = main[:, half * CM : (half + 1) * CM].reshape(8, H, CM)
            for m in range(4):
                ob[half, 2 * m, pl.ds(0, Q, stride=2), :] += side[m * Q : (m + 1) * Q, half * CM : (half + 1) * CM]
            img[pl.ds(k * 8, 8), :, half * CM : (half + 1) * CM] = ob[half].astype(BF16)
        image_out(k).start()

    loop(12, pass4)
    loop(12, lambda k: image_out(k).wait())

    def each(n, make):
        loop(n, lambda d: make(d + 1).start())
        loop(n, lambda d: make(d + 1).wait())

    def chunk(p):
        return pl.ds(pl.multiple_of(p * CHUNK, CHUNK), CHUNK)

    def piece(p):
        return pl.ds(pl.multiple_of(p * PIECE, PIECE), PIECE)

    ng = NR * NS

    def scatter1(d):
        peer = lax.rem(col + d, NC)
        return remote(s1.at[chunk(peer)], r1.at[col], sem1.at[0, d], sem1.at[1, d], {"col": peer})

    each(NC - 1, scatter1)
    r1[col] = s1[chunk(col), :]
    a1[...] = sum(r1[p].astype(F32) for p in range(NC))

    def scatter2(d):
        q = lax.rem(grp + d, ng)
        return remote(a1.at[piece(q)], r2.at[grp], sem2.at[0, d], sem2.at[1, d], grp_peer(d))

    each(ng - 1, scatter2)
    r2[grp] = a1[piece(grp), :]
    a3[piece(grp), :] = sum(r2[p] for p in range(ng)) * SCALE

    def gather3(d):
        return remote(a3.at[piece(grp)], a3.at[piece(grp)], sem3.at[0, d], sem3.at[1, d], grp_peer(d))

    each(ng - 1, gather3)
    s3[...] = a3[...].astype(BF16)
    r4[col] = s3[...]

    def gather4(d):
        return remote(s3, r4.at[col], sem4.at[0, d], sem4.at[1, d], col_peer(d))

    each(NC - 1, gather4)

    for p in range(NC):
        s5[p, 32:40, :] = jnp.zeros((8, CM), F32)
        if p < 5:
            s5[p, 32:33, :] = a_misc[p : p + 1, :]
    for half in range(2):
        t = a_wr[:, half * CM : (half + 1) * CM].T * SCALE
        for p in range(4):
            s5[half * 4 + p, 0:32, :] = t[p * 32 : (p + 1) * 32, :]

    def scatter5(d):
        peer = lax.rem(col + d, NC)
        return remote(s5.at[peer], r5.at[col], sem5.at[0, d], sem5.at[1, d], {"col": peer})

    each(NC - 1, scatter5)
    r5[col] = s5[col]
    a5[...] = sum(r5[p] for p in range(NC))
    r6[grp] = a5[...]

    def gather6(d):
        return remote(a5, r6.at[grp], sem6.at[0, d], sem6.at[1, d], grp_peer(d))

    each(ng - 1, gather6)
    a5[...] = sum(r6[p] for p in range(ng))
    r7[col] = a5[...]

    def gather7(d):
        return remote(a5, r7.at[col], sem7.at[0, d], sem7.at[1, d], col_peer(d))

    each(NC - 1, gather7)

    for p in range(3):
        o_spatial[p * CHUNK : (p + 1) * CHUNK, :] = r4[p].astype(F32)

    def summed(at, n):
        return r4[at // CHUNK, at % CHUNK : at % CHUNK + n, :].astype(F32)

    for q in range(4):
        o_expand[:, q * CM : (q + 1) * CM] = summed(1152 + q * 128, 128)
        for part in range(2):
            o_project[part * 128 : (part + 1) * 128, q * CM : (q + 1) * CM] = summed(1664 + q * 256 + part * 128, 128)
    for p in range(NC):
        o_reduce[p * 32 : (p + 1) * 32, :] = r7[p, 0:32, :]
    for k in range(4):
        column = jnp.sum(jnp.where(eye, r7[k, 32:33, :], 0.0), axis=1, keepdims=True)
        o_classify[k * CM : (k + 1) * CM, 0:1] = -column
        o_classify[k * CM : (k + 1) * CM, 1:2] = column
    o_loss[...] = r7[4, 32:33, 0:1]


def per_device(image, wr, ws, we, wp, wc, mask, label):
    vmem = pl.BlockSpec(memory_space=pltpu.VMEM)
    hbm = pl.BlockSpec(memory_space=pl.ANY)
    v = pltpu.VMEM
    dma = pltpu.SemaphoreType.DMA
    scratch = [
        v((H, H, CI), BF16),
        v((H, H, CM), F32),
        v((8, 8 + H, CM), F32),
        v((Q + 1, Q, 3 * CM), BF16),
        v((Q, Q, 3 * CM), BF16),
        v((Q, Q, CI), BF16),
        v((2, H, CM), F32),
        v((H, CM), F32),
        v((H, CM), BF16),
        v((H, CM), BF16),
        v((16, CM), BF16),
        v((H + 16, CM), F32),
        v((Q, 3 * CM), BF16),
        v((TB * Q, CM), F32),
        v((TB * Q, CM), BF16),
        v((TB * Q, CO), F32),
        v((TB * Q, CO), F32),
        v((2, TB * Q, CM), F32),
        v((3, 8, CO), F32),
        v((8, CO), F32),
        v((TB * Q, CO), BF16),
        v((Q * Q, CO), BF16),
        v((8, Q + 8, CM), F32),
        v((Q + 1, Q, 2 * CM), BF16),
        v((3, 2 * CM, 2 * CM), BF16),
        v((2, 8, Q, 2 * CM), F32),
        v((2, H, CM), F32),
        v((H, H, CM), BF16),
        v((Q, CM), BF16),
        v((16, CM), BF16),
        v((Q + 16, CM), F32),
        v((Q, 2 * CM), BF16),
        v((Q, CM), F32),
        v((2, 8, H, CM), F32),
        v((CM, 9 * CM), F32),
        v((CM, CO), F32),
        v((CI, CO), F32),
        v((CM, CI), F32),
        v((8, CM), F32),
        v((NC * CHUNK, CM), BF16),
        v((NC, CHUNK, CM), BF16),
        v((CHUNK, CM), F32),
        v((NR * NS, PIECE, CM), F32),
        v((CHUNK, CM), F32),
        v((CHUNK, CM), BF16),
        v((NC, CHUNK, CM), BF16),
        v((NC, 40, CM), F32),
        v((NC, 40, CM), F32),
        v((40, CM), F32),
        v((NR * NS, 40, CM), F32),
        v((NC, 40, CM), F32),
        dma((IMG_CHUNKS,)),
        dma((12,)),
        dma((6,)),
        dma((6,)),
        dma((2, NC)),
        dma((2, NR * NS)),
        dma((2, NR * NS)),
        dma((2, NC)),
        dma((2, NC)),
        dma((2, NR * NS)),
        dma((2, NC)),
    ]
    shapes = [image.shape, (CI, CM), (9 * CM, CM), (CM, CO), (CI, CO), (CO, 2), (1, 1)]
    out = pl.pallas_call(
        kernel,
        out_shape=[jax.ShapeDtypeStruct(s, BF16 if k == 0 else F32) for k, s in enumerate(shapes)],
        in_specs=[hbm] + [vmem] * 6 + [pl.BlockSpec(memory_space=pltpu.SMEM)],
        out_specs=[hbm] + [vmem] * 6,
        scratch_shapes=scratch,
        compiler_params=pltpu.CompilerParams(
            collective_id=0, has_side_effects=True, vmem_limit_bytes=56 * 1024 * 1024
        ),
        cost_estimate=pl.CostEstimate(flops=7_000_000_000, bytes_accessed=12_000_000, transcendentals=4_000_000),
    )(image, wr, ws.reshape(3, 3 * CM, CM), we, wp, wc, mask[0], label)
    grad_image, g_reduce, g_spatial, g_expand, g_project, g_classify, loss = out
    return grad_image, g_reduce, g_spatial.reshape(3, 3, CM, CM), g_expand, g_project, g_classify, loss[0, 0]


def solution(mesh):
    in_specs = (P("slide", "row", "col", None), P(), P(), P(), P(), P(), P("slide", None, None), P("slide"))
    out_specs = (P("slide", "row", "col", None), P(), P(), P(), P(), P(), P())
    return jax.shard_map(per_device, mesh=mesh, in_specs=in_specs, out_specs=out_specs, check_vma=False)
```

time: 304 us -> 139 us (0.46); the launches traced: 299 us -> 139 us
  Pallas kernels: 0 us -> 123 us
  local copies, waits for them, and re-layouts: 80.5 us -> 12.4 us
  blocking collectives: 67.2 us -> 0 us
  waiting for transfers between devices: 51.7 us -> 0 us
  other arithmetic: 37.7 us -> 0 us
  matrix products: 32.1 us -> 0 us
  between operations: 17 us -> 3.05 us
  starting transfers between devices: 12.7 us -> 0 us
    pallas_call x0 -> x1, Pallas kernels: none -> 123 us  [per_device(): pl.pallas_call(kernel, out_shape=[jax.ShapeDtypeStruct(s, BF16 if k == 0...]
    psum x1 -> x0, blocking collectives: 67.2 us -> none  [per_device(): lax.psum((grad_reduce, grad_spatial, grad_expand, grad_project, grad_clas...]
    psum x1 -> x0, waiting for transfers between devices: 48.5 us -> none  [per_device(): lax.psum((grad_reduce, grad_spatial, grad_expand, grad_project, grad_clas...]
    dot_general x15 -> x0, matrix products: 32.1 us -> none  [the longest x1 7.3 us: per_device(): jnp.einsum('hwd,cd->hwc', pre_reduce_grad, reduce_weight, preferred_eleme...]
    reshape x3 -> x0, local copies, waits for them, and re-layouts: 24.7 us -> none  [the longest x1 12.4 us: per_device(): side_full = jnp.pad(side_grad[:, None, :, None, :], ((0, 0), (0, 1), (0,...]
    another operation x3 -> x0, local copies, waits for them, and re-layouts: 14.2 us -> none  [the longest x1 8.05 us: per_device(): pixels.reshape(half_rows, 2, half_cols, 2, in_channels)[:, 0, :, 0]]
    slice x5 -> x0, local copies, waits for them, and re-layouts: 14.1 us -> none  [the longest x1 8.63 us: gather_taps(): grid_view[row_tap // 2:row_tap // 2 + out_rows, row_tap % 2, col_tap // 2...]
    reduce_sum x5 -> x0, other arithmetic: 13.7 us -> none  [the longest x2 9.69 us: normed(): values * lax.rsqrt(jnp.mean(values * values, axis=-1, keepdims=True) + EP...]
  transfers between devices with their start and end apart: 5 -> 0, of which waited for: 2 -> 0; matrix products, arithmetic and copies ran while one was open for 19% -> 0% of each run, Pallas kernels for 0% -> 0%
where the time goes in v1:
time: 139 us
  Pallas kernels  123 us (88%)
  local copies, waits for them, and re-layouts  12.4 us (9%)
  between operations  3.05 us (2%)
    pallas_call x1, Pallas kernels, per_device(): pl.pallas_call(kernel, out_shape=[jax.ShapeDtypeStruct(s, BF16 if k == 0...  123 us
    unnamed x16, local copies, waits for them, and re-layouts  12.4 us

profile of v1, /device:TPU:1, one launch (start us, length us, event | category | flops | bytes accessed | tf_op | source)
XLA Modules:
  0.0 138.7 jit_solution(14259486385511100008)
XLA Ops:
  1.3 1.3 copy.19
  2.6 1.5 %copy.15.wc = f32[512,2]{1,0:T(8,128)} copy(f32[512,2]{0,1:T(2,128)} %param.13) | data formatting | bytes 8192 | tf_op args[5]
  4.1 123.3 %shard_map.135 = (bf16[1,96,96,256]{3,2,1,0:T(8,128)(2,1)}, f32[256,128]{1,0:T(8,128)}, f32[1152,128]{1,0:T(8,128)}, f32[128,512]{1,0:T(8,128)}, f32[256,512]{1,...) custom-call(bf16[1,96,96,256]{3,2,1,0:T(8,128)(2,1)} %img_hbm.1, bf16[256,128]{1,0:T(8,128)(2,1)} %wr.1, ...), custom_call_target="tpu_custom_call" | custom-call | flops 7000000000 | bytes 12000000 | tf_op jit(solution)/shard_map/pallas_call | solution.py:545
  127.4 1.7 %copy.16 = f32[512,2]{0,1:T(2,128)} copy(f32[512,2]{1,0:T(8,128)} %get-tuple-element.26) | data formatting | bytes 8192
  129.0 0.0 copy-start.3
  129.0 0.0 copy-start
  129.0 0.0 copy-start.2
  129.0 0.0 copy-start.1
  129.1 5.0 %copy.27 = bf16[1,96,96,256]{3,2,1,0:T(8,128)(2,1)} copy(bf16[1,96,96,256]{3,2,1,0:T(8,128)(2,1)} %get-tuple-element.35) | data formatting | bytes 9437184
  134.0 0.0 copy-done.3
  134.0 0.7 copy.28
  134.7 0.0 copy-done
  134.7 0.8 copy.29
  135.5 0.0 copy-done.2
  135.5 0.7 copy.30
  136.2 0.0 copy-done.1
  136.2 0.8 copy.31
Async XLA Ops:
  129.0 5.0 %copy-start.3 = (f32[256,128]{1,0:T(8,128)S(1)}, f32[256,128]{1,0:T(8,128)}, u32[]{:S(2)}) copy-start(f32[256,128]{1,0:T(8,128)} %get-tuple-element.36) | copy-start | bytes 393220
  129.0 5.6 %copy-start = (f32[1152,128]{1,0:T(8,128)S(1)}, f32[1152,128]{1,0:T(8,128)}, u32[]{:S(2)}) copy-start(f32[1152,128]{1,0:T(8,128)} %get-tuple-element.16) | copy-start | bytes 1769476
  129.0 6.4 %copy-start.2 = (f32[128,512]{1,0:T(8,128)S(1)}, f32[128,512]{1,0:T(8,128)}, u32[]{:S(2)}) copy-start(f32[128,512]{1,0:T(8,128)} %get-tuple-element.38) | copy-start | bytes 786436
  129.0 7.1 %copy-start.1 = (f32[256,512]{1,0:T(8,128)S(1)}, f32[256,512]{1,0:T(8,128)}, u32[]{:S(2)}) copy-start(f32[256,512]{1,0:T(8,128)} %get-tuple-element.39) | copy-start | bytes 1572868

commit v2 on v1

--- a/solution.py
+++ b/solution.py
@@ -33,16 +33,16 @@
     return lax.dot_general(a, b, (((0,), (0,)), ((), ())), preferred_element_type=F32)
 
 
-def lane_mean(x, n):
-    return jnp.sum(x, axis=-1, keepdims=True) * (1.0 / n)
-
-
-def rms_scale(v, n):
-    return lax.rsqrt(lane_mean(v * v, n) + EPSILON)
-
-
-def act(v):
-    half = v * (0.5 * rms_scale(v, CM))
+def lane_mean(x, ones):
+    return dot(x.astype(BF16), ones)
+
+
+def rms_scale(v, ones):
+    return lax.rsqrt(lane_mean(v * v, ones) + EPSILON)
+
+
+def act(v, ones):
+    half = v * (0.5 * rms_scale(v, ones))
     return half * jnp.tanh(half) + half
 
 
@@ -51,11 +51,15 @@
     return (0.5 + 0.5 * t) * (1.0 + half * (1.0 - t))
 
 
-def act_vjp(v, g):
-    r = rms_scale(v, CM)
+def act_vjp(v, g, ones):
+    r = rms_scale(v, ones)
     n = v * r
     dn = g * silu_slope(0.5 * n)
-    return r * (dn - n * lane_mean(dn * n, CM))
+    return r * (dn - n * lane_mean(dn * n, ones))
+
+
+def lanes(k):
+    return slice(k * CM, (k + 1) * CM)
 
 
 def loop(n, body):
@@ -70,10 +74,10 @@
     img_hbm, wr, ws, we, wp, wc, mask, label,
     gimg_hbm, o_reduce, o_spatial, o_expand, o_project, o_classify, o_loss,
     img, pre, actb, rc_odd, rc_even, evp, evb, colb, col16, hcol, hcor, hcolf, srow,
-    psp, spat, ne, npj, rs, feat, gb, eg, pg, dbuf, dcat, wback, eo, natb, prg16,
+    psp, spat, ne, npj, r_e, r_p, feat, gb, dnb, eg, pg, dbuf, dcat, wback, eo, natb, prg16,
     dright, dcor, drightf, drow, dcol, ob,
     a_ws, a_we, a_wp, a_wr, a_misc,
-    s1, r1, a1, r2, a3, s3, r4, s5, r5, a5, r6, r7,
+    s1, r1, a1, r2, a3, s3, r4, s5, r5, a5, r6, a7, r7,
     sem_in, sem_out, sem_h, sem_g, sem1, sem2, sem3, sem4, sem5, sem6, sem7,
 ):
     row, col, sld = lax.axis_index("row"), lax.axis_index("col"), lax.axis_index("slide")
@@ -122,6 +126,8 @@
         wback[slot, CM : 2 * CM, CM : 2 * CM] = tap(a, 0)
     actb[:, 0:8, :] = jnp.zeros_like(actb[:, 0:8, :])
     dbuf[:, Q : Q + 8, :] = jnp.zeros_like(dbuf[:, Q : Q + 8, :])
+    ones_m = jnp.full((CM, CM), 1.0 / CM, BF16)
+    ones_o = jnp.full((CM, CM), 1.0 / CO, BF16)
     a_ws[...] = jnp.zeros_like(a_ws)
     a_we[...] = jnp.zeros_like(a_we)
     a_wp[...] = jnp.zeros_like(a_wp)
@@ -152,29 +158,19 @@
     def _():
         dcor[...] = jnp.zeros_like(dcor)
 
-    eye = (
-        lax.broadcasted_iota(jnp.int32, (CM, CM), 0) == lax.broadcasted_iota(jnp.int32, (CM, CM), 1)
-    )
-    wdiff = wc[:, 1:2] - wc[:, 0:1]
-    drow_w = jnp.concatenate(
-        [
-            jnp.sum(jnp.where(eye, wdiff[k * CM : (k + 1) * CM], 0.0), axis=0, keepdims=True)
-            for k in range(CO // CM)
-        ],
-        axis=1,
-    )
+    drow_w = wc[1:2, :] - wc[0:1, :]
     sign = 1.0 - 2.0 * label[0].astype(F32)
     tissue_all = mask[...].astype(F32)
-    tiles = jnp.sum(jnp.sum(tissue_all, axis=1, keepdims=True), axis=0, keepdims=True)
+    tiles = jnp.sum(jnp.sum(tissue_all, axis=0), axis=1, keepdims=True)
     mask_r = lax.broadcasted_iota(jnp.int32, mask.shape, 0)
-    mask_c = lax.broadcasted_iota(jnp.int32, mask.shape, 1)
+    mask_c = lax.broadcasted_iota(jnp.int32, mask.shape, 2)
 
     def pass1(k):
         image_copy(k).wait()
         x = img[pl.ds(k * 8, 8)].reshape(8 * H, CI)
         v = dot(x, wr[...])
         pre[pl.ds(k * 8, 8)] = v.reshape(8, H, CM)
-        actb[:, 8 : 8 + H, :] = act(v).reshape(8, H, CM)
+        actb[:, 8 : 8 + H, :] = act(v, ones_m).reshape(8, H, CM)
         for r in range(8):
             rows, at = (rc_even, k * 4 + r // 2) if r % 2 == 0 else (rc_odd, k * 4 + r // 2 + 1)
             for b in range(3):
@@ -212,6 +208,14 @@
 
     loop(Q, even_rows)
 
+    def project(b):
+        at = pl.ds(b * 8 * Q, 8 * Q)
+        p = dot(evp[pl.ds(b * 8, 8)].reshape(8 * Q, CI), wp[...])
+        npj[at, :] = p
+        r_p[at, :] = lax.rsqrt(lane_mean(sum(p[:, lanes(k)] * p[:, lanes(k)] for k in range(4)), ones_o) + EPSILON)
+
+    loop(6, project)
+
     for copy, sends, takes in forward:
         pl.when(takes)(copy.wait_recv)
         pl.when(sends)(copy.wait_send)
@@ -234,62 +238,74 @@
 
     npx = TB * Q
 
+    def taps(a, at, n):
+        if a == 1:
+            return rc_even[pl.ds(at, n)].reshape(n * Q, 3 * CM)
+        return rc_odd[pl.ds(at + a // 2, n)].reshape(n * Q, 3 * CM)
+
     def tile_row(u):
         i0 = u * TB
-
-        def taps(a, at, n):
-            if a == 1:
-                return rc_even[pl.ds(at, n)].reshape(n * Q, 3 * CM)
-            return rc_odd[pl.ds(at + a // 2, n)].reshape(n * Q, 3 * CM)
 
         def convolve(b):
             at = i0 + b * 8
             v = sum(dot(taps(a, at, 8), ws[a]) for a in range(3))
             psp[pl.ds(b * 8 * Q, 8 * Q), :] = v
-            spat[pl.ds(b * 8 * Q, 8 * Q), :] = act(v).astype(BF16)
+            spat[pl.ds(b * 8 * Q, 8 * Q), :] = act(v, ones_m).astype(BF16)
 
         loop(2, convolve)
-        ne[...] = dot(spat[...], we[...])
-        npj[...] = dot(evp[pl.ds(i0, TB)].reshape(npx, CI), wp[...])
+
+        def expand(b):
+            at = pl.ds(b * 8 * Q, 8 * Q)
+            e = dot(spat[at, :], we[...])
+            ne[at, :] = e
+            r_e[at, :] = lax.rsqrt(lane_mean(sum(e[:, lanes(k)] * e[:, lanes(k)] for k in range(4)), ones_o) + EPSILON)
+
+        loop(2, expand)
         feat[...] = jnp.zeros_like(feat)
 
-        def merge(i):
-            for v in range(3):
-                at = pl.ds(i * Q + v * TB, TB)
-                e, p = ne[at, :], npj[at, :]
-                r_e, r_p = rms_scale(e, CO), rms_scale(p, CO)
-                n_e, n_p = e * r_e, p * r_p
-                ne[at, :], npj[at, :] = n_e, n_p
-                rs[0, at, :], rs[1, at, :] = (jnp.broadcast_to(r, (TB, CM)) for r in (r_e, r_p))
-                half = 0.5 * (n_e + n_p)
+        def merge(b):
+            at = pl.ds(b * 4 * Q, 4 * Q)
+            out = pl.ds(i0 * Q + b * 4 * Q, 4 * Q)
+            h_e, h_p = 0.5 * r_e[at, :], 0.5 * r_p[out, :]
+            for k in range(4):
+                half = ne[at, lanes(k)] * h_e + npj[out, lanes(k)] * h_p
                 merged = half * jnp.tanh(half) + half
-                feat[v] += merged[0:8] + merged[8:16]
-
-        loop(TB, merge)
+                feat[:, lanes(k)] += jnp.sum(merged.reshape(4, Q, CM), axis=0)
+
+        loop(4, merge)
 
         for v in range(3):
-            f = jnp.sum(feat[v], axis=0, keepdims=True) * (1.0 / (TB * TB))
+            f = jnp.sum(feat[v * TB : (v + 1) * TB, :], axis=0, keepdims=True) * (1.0 / (TB * TB))
             margin = jnp.sum(f * drow_w, axis=1, keepdims=True) * sign
             here = (mask_r == row * 3 + u) & (mask_c == col * 3 + v)
             tissue = jnp.where(here, tissue_all, 0.0)
-            tissue = jnp.sum(jnp.sum(tissue, axis=1, keepdims=True), axis=0, keepdims=True)
+            tissue = jnp.sum(jnp.sum(tissue, axis=0), axis=1, keepdims=True)
             soft = jnp.maximum(margin, 0.0) + jnp.log(1.0 + jnp.exp(-jnp.abs(margin)))
             weight = tissue * (0.5 + 0.5 * jnp.tanh(0.5 * margin)) / tiles * sign
             for k in range(CO // CM):
                 a_misc[k : k + 1, :] += f[:, k * CM : (k + 1) * CM] * weight
             a_misc[4:5, :] += jnp.broadcast_to(tissue * soft / tiles, (1, CM))
-            gb[v : v + 1, :] = drow_w * (weight * 288.0)
-
-        def unmerge(i):
-            for v in range(3):
-                at = pl.ds(i * Q + v * TB, TB)
-                n_e, n_p = ne[at, :], npj[at, :]
-                dn = gb[v : v + 1, :] * silu_slope(0.5 * (n_e + n_p))
-                out = pl.ds(i0 * Q + i * Q + v * TB, TB)
-                eg[at, :] = (rs[0, at, 0:1] * (dn - n_e * lane_mean(dn * n_e, CO))).astype(BF16)
-                pg[out, :] = (rs[1, at, 0:1] * (dn - n_p * lane_mean(dn * n_p, CO))).astype(BF16)
-
-        loop(TB, unmerge)
+            gb[v * TB : (v + 1) * TB, :] = jnp.broadcast_to(drow_w * (weight * 288.0), (TB, CO))
+
+        def unmerge(b):
+            at = pl.ds(b * 4 * Q, 4 * Q)
+            out = pl.ds(i0 * Q + b * 4 * Q, 4 * Q)
+            s_e, s_p = r_e[at, :], r_p[out, :]
+            z_e, z_p = 0.0, 0.0
+            for k in range(4):
+                n_e, n_p = ne[at, lanes(k)] * s_e, npj[out, lanes(k)] * s_p
+                slope = silu_slope(0.5 * (n_e + n_p)).reshape(4, Q, CM)
+                dn = (slope * gb[:, lanes(k)][None]).reshape(4 * Q, CM)
+                dnb[:, lanes(k)] = dn
+                z_e, z_p = z_e + dn * n_e, z_p + dn * n_p
+            m_e, m_p = lane_mean(z_e, ones_o), lane_mean(z_p, ones_o)
+            for k in range(4):
+                dn = dnb[:, lanes(k)]
+                n_e, n_p = ne[at, lanes(k)] * s_e, npj[out, lanes(k)] * s_p
+                eg[at, lanes(k)] = (s_e * (dn - n_e * m_e)).astype(BF16)
+                pg[out, lanes(k)] = (s_p * (dn - n_p * m_p)).astype(BF16)
+
+        loop(4, unmerge)
 
         a_we[...] += dot_tn(spat[...], eg[...])
         a_wp[...] += dot_tn(evp[pl.ds(i0, TB)].reshape(npx, CI), pg[pl.ds(i0 * Q, npx), :])
@@ -297,15 +313,13 @@
         def unconvolve(b):
             at = pl.ds(b * 8 * Q, 8 * Q)
             g = dot_nt(eg[at, :], we[...])
-            d = act_vjp(psp[at, :], g)
+            d = act_vjp(psp[at, :], g, ones_m)
             dbuf[:, 0:Q, :] = d.reshape(8, Q, CM)
             d16 = d.astype(BF16)
             dcat[pl.ds(i0 + b * 8, 8), :, 0:CM] = d16.reshape(8, Q, CM)
             for r in range(8):
                 dcat[i0 + b * 8 + r, :, CM : 2 * CM] = dbuf[r, 1 : Q + 1, :].astype(BF16)
                 dcol[pl.ds(i0 + b * 8 + r, 1), :] = dbuf[r, 0:1, :]
-            for a in range(3):
-                a_ws[:, a * 3 * CM : (a + 1) * 3 * CM] += dot_tn(d16, taps(a, i0 + b * 8, 8))
 
         loop(2, unconvolve)
 
@@ -323,6 +337,13 @@
     for copy, sends, _ in backward:
         pl.when(sends)(copy.start)
 
+    def spatial_weight_grad(u):
+        d16 = dcat[pl.ds(u * TB, TB), :, 0:CM].reshape(npx, CM)
+        for a in range(3):
+            a_ws[:, a * 3 * CM : (a + 1) * 3 * CM] += dot_tn(d16, taps(a, u * TB, TB))
+
+    loop(3, spatial_weight_grad)
+
     for t in range(9):
         s1[t * CM : (t + 1) * CM, :] = a_ws[:, t * CM : (t + 1) * CM].T.astype(BF16)
     for q in range(4):
@@ -330,6 +351,46 @@
         s1[1664 + q * 256 : 1664 + (q + 1) * 256, :] = a_wp[:, q * CM : (q + 1) * CM].astype(BF16)
     s1[2688:3072, :] = jnp.zeros((384, CM), BF16)
 
+    ng = NR * NS
+
+    def start(n, make):
+        loop(n, lambda d: make(d + 1).start())
+
+    def finish(n, make):
+        loop(n, lambda d: make(d + 1).wait())
+
+    def chunk(p):
+        return pl.ds(pl.multiple_of(p * CHUNK, CHUNK), CHUNK)
+
+    def piece(p):
+        return pl.ds(pl.multiple_of(p * PIECE, PIECE), PIECE)
+
+    def scatter1(d):
+        peer = lax.rem(col + d, NC)
+        return remote(s1.at[chunk(peer)], r1.at[col], sem1.at[0, d], sem1.at[1, d], {"col": peer})
+
+    def scatter2(d):
+        q = lax.rem(grp + d, ng)
+        return remote(a1.at[piece(q)], r2.at[grp], sem2.at[0, d], sem2.at[1, d], grp_peer(d))
+
+    def gather3(d):
+        return remote(a3.at[piece(grp)], a3.at[piece(grp)], sem3.at[0, d], sem3.at[1, d], grp_peer(d))
+
+    def gather4(d):
+        return remote(s3, r4.at[col], sem4.at[0, d], sem4.at[1, d], col_peer(d))
+
+    def scatter5(d):
+        peer = lax.rem(col + d, NC)
+        return remote(s5.at[peer], r5.at[col], sem5.at[0, d], sem5.at[1, d], {"col": peer})
+
+    def gather6(d):
+        return remote(a5, r6.at[grp], sem6.at[0, d], sem6.at[1, d], grp_peer(d))
+
+    def gather7(d):
+        return remote(a7, r7.at[col], sem7.at[0, d], sem7.at[1, d], col_peer(d))
+
+    start(NC - 1, scatter1)
+
     for copy, sends, takes in backward:
         pl.when(takes)(copy.wait_recv)
         pl.when(sends)(copy.wait_send)
@@ -352,106 +413,79 @@
         eo[0] = dot_nt(here, wback[0]).reshape(8, Q, 2 * CM)
         eo[1] = (dot_nt(here, wback[1]) + dot_nt(below, wback[2])).reshape(8, Q, 2 * CM)
 
-        def one_row(i):
+        def some_rows(c):
             for rp in range(2):
-                at = 2 * (i0 + i) + rp
+                at = 2 * (i0 + 4 * c)
                 for cp in range(2):
-                    v = pre[at, pl.ds(cp, Q, stride=2), :]
-                    natb[rp, pl.ds(cp, Q, stride=2), :] = act_vjp(v, eo[rp, i, :, cp * CM : (cp + 1) * CM])
-                prg16[at] = natb[rp].astype(BF16)
-
-        loop(8, one_row)
+                    v = jnp.concatenate([pre[at + 2 * i + rp, pl.ds(cp, Q, stride=2), :] for i in range(4)], axis=0)
+                    g = eo[rp, pl.ds(4 * c, 4), :, lanes(cp)].reshape(4 * Q, CM)
+                    d = act_vjp(v, g, ones_m)
+                    for i in range(4):
+                        natb[rp, i, pl.ds(cp, Q, stride=2), :] = d[i * Q : (i + 1) * Q]
+                for i in range(4):
+                    prg16[at + 2 * i + rp] = natb[rp, i].astype(BF16)
+
+        loop(2, some_rows)
         rows = pl.ds(2 * i0, 16)
         a_wr[...] += dot_tn(prg16[rows].reshape(16 * H, CM), img[rows].reshape(16 * H, CI))
 
     loop(6, pass3)
 
-    def image_out(k):
-        rows = pl.ds(k * 8, 8)
-        return pltpu.make_async_copy(img.at[rows], gimg_hbm.at[0, rows], sem_out.at[k])
-
-    def pass4(k):
-        main = dot_nt(prg16[pl.ds(k * 8, 8)].reshape(8 * H, CM), wr[...])
-        side = dot_nt(pg[pl.ds(k * 4 * Q, 4 * Q), :], wp[...])
-        for half in range(2):
-            ob[half] = main[:, half * CM : (half + 1) * CM].reshape(8, H, CM)
-            for m in range(4):
-                ob[half, 2 * m, pl.ds(0, Q, stride=2), :] += side[m * Q : (m + 1) * Q, half * CM : (half + 1) * CM]
-            img[pl.ds(k * 8, 8), :, half * CM : (half + 1) * CM] = ob[half].astype(BF16)
-        image_out(k).start()
-
-    loop(12, pass4)
-    loop(12, lambda k: image_out(k).wait())
-
-    def each(n, make):
-        loop(n, lambda d: make(d + 1).start())
-        loop(n, lambda d: make(d + 1).wait())
-
-    def chunk(p):
-        return pl.ds(pl.multiple_of(p * CHUNK, CHUNK), CHUNK)
-
-    def piece(p):
-        return pl.ds(pl.multiple_of(p * PIECE, PIECE), PIECE)
-
-    ng = NR * NS
-
-    def scatter1(d):
-        peer = lax.rem(col + d, NC)
-        return remote(s1.at[chunk(peer)], r1.at[col], sem1.at[0, d], sem1.at[1, d], {"col": peer})
-
-    each(NC - 1, scatter1)
+    finish(NC - 1, scatter1)
     r1[col] = s1[chunk(col), :]
     a1[...] = sum(r1[p].astype(F32) for p in range(NC))
-
-    def scatter2(d):
-        q = lax.rem(grp + d, ng)
-        return remote(a1.at[piece(q)], r2.at[grp], sem2.at[0, d], sem2.at[1, d], grp_peer(d))
-
-    each(ng - 1, scatter2)
-    r2[grp] = a1[piece(grp), :]
-    a3[piece(grp), :] = sum(r2[p] for p in range(ng)) * SCALE
-
-    def gather3(d):
-        return remote(a3.at[piece(grp)], a3.at[piece(grp)], sem3.at[0, d], sem3.at[1, d], grp_peer(d))
-
-    each(ng - 1, gather3)
-    s3[...] = a3[...].astype(BF16)
-    r4[col] = s3[...]
-
-    def gather4(d):
-        return remote(s3, r4.at[col], sem4.at[0, d], sem4.at[1, d], col_peer(d))
-
-    each(NC - 1, gather4)
+    start(ng - 1, scatter2)
 
     for p in range(NC):
         s5[p, 32:40, :] = jnp.zeros((8, CM), F32)
         if p < 5:
             s5[p, 32:33, :] = a_misc[p : p + 1, :]
     for half in range(2):
-        t = a_wr[:, half * CM : (half + 1) * CM].T * SCALE
+        t = a_wr[:, lanes(half)].T * SCALE
         for p in range(4):
             s5[half * 4 + p, 0:32, :] = t[p * 32 : (p + 1) * 32, :]
-
-    def scatter5(d):
-        peer = lax.rem(col + d, NC)
-        return remote(s5.at[peer], r5.at[col], sem5.at[0, d], sem5.at[1, d], {"col": peer})
-
-    each(NC - 1, scatter5)
+    start(NC - 1, scatter5)
+
+    def image_out(k):
+        rows = pl.ds(k * 8, 8)
+        return pltpu.make_async_copy(img.at[rows], gimg_hbm.at[0, rows], sem_out.at[k])
+
+    def pass4(k):
+        main = dot_nt(prg16[pl.ds(k * 8, 8)].reshape(8 * H, CM), wr[...])
+        side = dot_nt(pg[pl.ds(k * 4 * Q, 4 * Q), :], wp[...])
+        for m in range(4):
+            at = k * 8 + 2 * m
+            for half in range(2):
+                ob[half, m] = main[2 * m * H : (2 * m + 1) * H, lanes(half)]
+                ob[half, m, pl.ds(0, Q, stride=2), :] += side[m * Q : (m + 1) * Q, lanes(half)]
+                gimg_hbm[0, at, :, lanes(half)] = ob[half, m].astype(BF16)
+            gimg_hbm[0, at + 1] = main[(2 * m + 1) * H : (2 * m + 2) * H].astype(BF16)
+
+    def some(lo, hi):
+        loop(hi - lo, lambda k: pass4(lo + k))
+
+    some(0, 4)
+    finish(ng - 1, scatter2)
+    r2[grp] = a1[piece(grp), :]
+    a3[piece(grp), :] = sum(r2[p] for p in range(ng)) * SCALE
+    start(ng - 1, gather3)
+    finish(NC - 1, scatter5)
     r5[col] = s5[col]
     a5[...] = sum(r5[p] for p in range(NC))
     r6[grp] = a5[...]
-
-    def gather6(d):
-        return remote(a5, r6.at[grp], sem6.at[0, d], sem6.at[1, d], grp_peer(d))
-
-    each(ng - 1, gather6)
-    a5[...] = sum(r6[p] for p in range(ng))
-    r7[col] = a5[...]
-
-    def gather7(d):
-        return remote(a5, r7.at[col], sem7.at[0, d], sem7.at[1, d], col_peer(d))
-
-    each(NC - 1, gather7)
+    start(ng - 1, gather6)
+    some(4, 8)
+    finish(ng - 1, gather3)
+    s3[...] = a3[...].astype(BF16)
+    r4[col] = s3[...]
+    start(NC - 1, gather4)
+    finish(ng - 1, gather6)
+    a7[...] = sum(r6[p] for p in range(ng))
+    r7[col] = a7[...]
+    start(NC - 1, gather7)
+    some(8, 12)
+    finish(NC - 1, gather4)
+    finish(NC - 1, gather7)
 
     for p in range(3):
         o_spatial[p * CHUNK : (p + 1) * CHUNK, :] = r4[p].astype(F32)
@@ -466,10 +500,19 @@
     for p in range(NC):
         o_reduce[p * 32 : (p + 1) * 32, :] = r7[p, 0:32, :]
     for k in range(4):
-        column = jnp.sum(jnp.where(eye, r7[k, 32:33, :], 0.0), axis=1, keepdims=True)
-        o_classify[k * CM : (k + 1) * CM, 0:1] = -column
-        o_classify[k * CM : (k + 1) * CM, 1:2] = column
+        o_classify[0:1, lanes(k)] = -r7[k, 32:33, :]
+        o_classify[1:2, lanes(k)] = r7[k, 32:33, :]
     o_loss[...] = r7[4, 32:33, 0:1]
+
+
+def hand_over(*refs):
+    n = (len(refs) - 1) // 2
+    given, taken, sem = refs[:n], refs[n : 2 * n], refs[-1]
+    copies = [pltpu.make_async_copy(a, b, sem.at[k]) for k, (a, b) in enumerate(zip(given, taken))]
+    for c in copies:
+        c.start()
+    for c in copies:
+        c.wait()
 
 
 def per_device(image, wr, ws, we, wp, wc, mask, label):
@@ -494,24 +537,26 @@
         v((TB * Q, CM), F32),
         v((TB * Q, CM), BF16),
         v((TB * Q, CO), F32),
-        v((TB * Q, CO), F32),
-        v((2, TB * Q, CM), F32),
-        v((3, 8, CO), F32),
-        v((8, CO), F32),
+        v((Q * Q, CO), F32),
+        v((TB * Q, CM), F32),
+        v((Q * Q, CM), F32),
+        v((Q, CO), F32),
+        v((Q, CO), F32),
+        v((4 * Q, CO), F32),
         v((TB * Q, CO), BF16),
         v((Q * Q, CO), BF16),
         v((8, Q + 8, CM), F32),
         v((Q + 1, Q, 2 * CM), BF16),
         v((3, 2 * CM, 2 * CM), BF16),
         v((2, 8, Q, 2 * CM), F32),
-        v((2, H, CM), F32),
+        v((2, 4, H, CM), F32),
         v((H, H, CM), BF16),
         v((Q, CM), BF16),
         v((16, CM), BF16),
         v((Q + 16, CM), F32),
         v((Q, 2 * CM), BF16),
         v((Q, CM), F32),
-        v((2, 8, H, CM), F32),
+        v((2, 4, H, CM), F32),
         v((CM, 9 * CM), F32),
         v((CM, CO), F32),
         v((CI, CO), F32),
@@ -528,6 +573,7 @@
         v((NC, 40, CM), F32),
         v((40, CM), F32),
         v((NR * NS, 40, CM), F32),
+        v((40, CM), F32),
         v((NC, 40, CM), F32),
         dma((IMG_CHUNKS,)),
         dma((12,)),
@@ -541,20 +587,28 @@
         dma((2, NR * NS)),
         dma((2, NC)),
     ]
-    shapes = [image.shape, (CI, CM), (9 * CM, CM), (CM, CO), (CI, CO), (CO, 2), (1, 1)]
+    shapes = [image.shape, (CI, CM), (9 * CM, CM), (CM, CO), (CI, CO), (2, CO), (1, 1)]
     out = pl.pallas_call(
         kernel,
-        out_shape=[jax.ShapeDtypeStruct(s, BF16 if k == 0 else F32) for k, s in enumerate(shapes)],
+        out_shape=[v(s, BF16 if k == 0 else F32) for k, s in enumerate(shapes)],
         in_specs=[hbm] + [vmem] * 6 + [pl.BlockSpec(memory_space=pltpu.SMEM)],
-        out_specs=[hbm] + [vmem] * 6,
+        out_specs=[vmem] * 7,
         scratch_shapes=scratch,
         compiler_params=pltpu.CompilerParams(
-            collective_id=0, has_side_effects=True, vmem_limit_bytes=56 * 1024 * 1024
+            collective_id=0, has_side_effects=True, vmem_limit_bytes=50 * 1024 * 1024
         ),
         cost_estimate=pl.CostEstimate(flops=7_000_000_000, bytes_accessed=12_000_000, transcendentals=4_000_000),
-    )(image, wr, ws.reshape(3, 3 * CM, CM), we, wp, wc, mask[0], label)
+    )(image, wr, ws.reshape(3, 3 * CM, CM), we, wp, wc.T, jnp.transpose(mask, (1, 0, 2)), label)
+    out = pl.pallas_call(
+        hand_over,
+        out_shape=[jax.ShapeDtypeStruct(o.shape, o.dtype) for o in out],
+        in_specs=[vmem] * len(out),
+        out_specs=[hbm] * len(out),
+        scratch_shapes=[dma((len(out),))],
+        compiler_params=pltpu.CompilerParams(vmem_limit_bytes=1024 * 1024),
+    )(*out)
     grad_image, g_reduce, g_spatial, g_expand, g_project, g_classify, loss = out
-    return grad_image, g_reduce, g_spatial.reshape(3, 3, CM, CM), g_expand, g_project, g_classify, loss[0, 0]
+    return grad_image, g_reduce, g_spatial.reshape(3, 3, CM, CM), g_expand, g_project, g_classify.T, loss[0, 0]
 
 
 def solution(mesh):

time: 139 us -> 77.2 us (0.56)
  Pallas kernels: 123 us -> 75.7 us
  local copies, waits for them, and re-layouts: 12.4 us -> 0 us
  between operations: 3.05 us -> 1.29 us
    pallas_call x1 -> x2, Pallas kernels: 123 us -> 75.7 us  [the longest x1 72.4 us: per_device(): pl.pallas_call(kernel, out_shape=[v(s, BF16 if k == 0 else F32) for k, s...]
    unnamed x16 -> x0, local copies, waits for them, and re-layouts: 12.4 us -> none
where the time goes in v2:
time: 77.2 us; the launch traced here: 77 us
  Pallas kernels  75.7 us (98%)
  between operations  1.29 us (2%)
    pallas_call x1, Pallas kernels, per_device(): pl.pallas_call(kernel, out_shape=[v(s, BF16 if k == 0 else F32) for k, s...  72.4 us
    pallas_call x1, Pallas kernels, per_device(): pl.pallas_call(hand_over, out_shape=[jax.ShapeDtypeStruct(o.shape, o.dtyp...  3.34 us

profile of v2, /device:TPU:1, one launch (start us, length us, event | category | flops | bytes accessed | tf_op | source)
XLA Modules:
  0.0 77.0 jit_solution(5473340156975442010)
XLA Ops:
  1.3 72.4 %shard_map.135 = (bf16[1,96,96,256]{3,2,1,0:T(8,128)(2,1)S(1)}, f32[256,128]{1,0:T(8,128)S(1)}, f32[1152,128]{1,0:T(8,128)S(1)}, f32[128,512]{1,0:T(8,128)S(1)},...) custom-call(bf16[1,96,96,256]{3,2,1,0:T(8,128)(2,1)} %img_hbm.1, bf16[256,128]{1,0:T(8,128)(2,1)} %wr.1, ...), custom_call_target="tpu_custom_call" | custom-call | flops 7000000000 | bytes 12000000 | tf_op jit(solution)/shard_map/pallas_call | solution.py:591
  73.7 3.3 %shard_map.136 = (bf16[1,96,96,256]{3,2,1,0:T(8,128)(2,1)}, f32[256,128]{1,0:T(8,128)}, f32[1152,128]{1,0:T(8,128)}, f32[128,512]{1,0:T(8,128)}, f32[256,512]{1,...) custom-call(bf16[1,96,96,256]{3,2,1,0:T(8,128)(2,1)S(1)} %get-tuple-element.21.refs_0_, ...), custom_call_target="tpu_custom_call" | custom-call | tf_op jit(solution)/shard_map/pallas_call | solution.py:602

commit v3 on v2

--- a/solution.py
+++ b/solution.py
@@ -37,25 +37,22 @@
     return dot(x.astype(BF16), ones)
 
 
-def rms_scale(v, ones):
-    return lax.rsqrt(lane_mean(v * v, ones) + EPSILON)
-
-
-def act(v, ones):
-    half = v * (0.5 * rms_scale(v, ones))
+def half_scale(squares, ones):
+    return lax.rsqrt(lane_mean(squares, ones) + 4.0 * EPSILON)
+
+
+def silu_vjp(half, g):
+    t = jnp.tanh(half)
+    return g * (1.0 + t) * (1.0 + half * (1.0 - t))
+
+
+def silu(half):
     return half * jnp.tanh(half) + half
 
 
-def silu_slope(half):
-    t = jnp.tanh(half)
-    return (0.5 + 0.5 * t) * (1.0 + half * (1.0 - t))
-
-
-def act_vjp(v, g, ones):
-    r = rms_scale(v, ones)
-    n = v * r
-    dn = g * silu_slope(0.5 * n)
-    return r * (dn - n * lane_mean(dn * n, ones))
+def act_vjp(half, scale, g, ones):
+    dn = silu_vjp(half, g)
+    return scale * (dn - half * lane_mean(dn * half, ones))
 
 
 def lanes(k):
@@ -70,15 +67,20 @@
     lax.fori_loop(0, n, step, 0)
 
 
+def unrolled(n, body):
+    for i in range(n):
+        body(i)
+
+
 def kernel(
-    img_hbm, wr, ws, we, wp, wc, mask, label,
+    img_hbm, wr_hbm, ws_hbm, we_hbm, wp_hbm, wc, mask, label,
     gimg_hbm, o_reduce, o_spatial, o_expand, o_project, o_classify, o_loss,
-    img, pre, actb, rc_odd, rc_even, evp, evb, colb, col16, hcol, hcor, hcolf, srow,
+    wr, ws, we, wp, img, pre, prs, actb, rc_odd, rc_even, evp, evb, colb, col16, hcol, hcor, hcolf, srow,
     psp, spat, ne, npj, r_e, r_p, feat, gb, dnb, eg, pg, dbuf, dcat, wback, eo, natb, prg16,
     dright, dcor, drightf, drow, dcol, ob,
     a_ws, a_we, a_wp, a_wr, a_misc,
-    s1, r1, a1, r2, a3, s3, r4, s5, r5, a5, r6, a7, r7,
-    sem_in, sem_out, sem_h, sem_g, sem1, sem2, sem3, sem4, sem5, sem6, sem7,
+    s1, r0, r1, a1, r2, a3, s3, r4, s5, r5, a5, r6, a7, r7,
+    sem_in, sem_w, sem_h, sem_g, sem0, sem1, sem2, sem3, sem4, sem5, sem6, sem7, sem8,
 ):
     row, col, sld = lax.axis_index("row"), lax.axis_index("col"), lax.axis_index("slide")
     grp = row * NS + sld
@@ -92,7 +94,14 @@
             img_hbm.at[0, pl.ds(k * rows_in, rows_in)], img.at[pl.ds(k * rows_in, rows_in)], sem_in.at[k]
         )
 
+    weights = [
+        pltpu.make_async_copy(a, b, sem_w.at[k])
+        for k, (a, b) in enumerate(((wr_hbm, wr), (ws_hbm, ws), (we_hbm, we), (wp_hbm, wp)))
+    ]
+    weights[0].start()
     loop(IMG_CHUNKS, lambda k: image_copy(k).start())
+    for copy in weights[1:]:
+        copy.start()
 
     def col_peer(d):
         return {"col": lax.rem(col + d, NC)}
@@ -115,19 +124,10 @@
     def _():
         pl.semaphore_signal(barrier, inc=1, device_id={"row": row - 1, "col": col - 1}, device_id_type=MESH)
 
-    wback[...] = jnp.zeros_like(wback)
-
-    def tap(a, b):
-        return ws[a, b * CM : (b + 1) * CM, :]
-
-    for slot, a in ((0, 1), (1, 2), (2, 0)):
-        wback[slot, 0:CM, 0:CM] = tap(a, 1)
-        wback[slot, CM : 2 * CM, 0:CM] = tap(a, 2)
-        wback[slot, CM : 2 * CM, CM : 2 * CM] = tap(a, 0)
     actb[:, 0:8, :] = jnp.zeros_like(actb[:, 0:8, :])
     dbuf[:, Q : Q + 8, :] = jnp.zeros_like(dbuf[:, Q : Q + 8, :])
-    ones_m = jnp.full((CM, CM), 1.0 / CM, BF16)
-    ones_o = jnp.full((CM, CM), 1.0 / CO, BF16)
+    ones_m = jnp.full((CM, CM), 4.0 / CM, BF16)
+    ones_o = jnp.full((CM, CM), 4.0 / CO, BF16)
     a_ws[...] = jnp.zeros_like(a_ws)
     a_we[...] = jnp.zeros_like(a_we)
     a_wp[...] = jnp.zeros_like(a_wp)
@@ -165,12 +165,17 @@
     mask_r = lax.broadcasted_iota(jnp.int32, mask.shape, 0)
     mask_c = lax.broadcasted_iota(jnp.int32, mask.shape, 2)
 
+    weights[0].wait()
+
     def pass1(k):
         image_copy(k).wait()
         x = img[pl.ds(k * 8, 8)].reshape(8 * H, CI)
         v = dot(x, wr[...])
-        pre[pl.ds(k * 8, 8)] = v.reshape(8, H, CM)
-        actb[:, 8 : 8 + H, :] = act(v, ones_m).reshape(8, H, CM)
+        scale = half_scale(v * v, ones_m)
+        half = v * scale
+        pre[pl.ds(k * 8, 8)] = half.reshape(8, H, CM)
+        prs[pl.ds(k * 8, 8)] = scale.reshape(8, H, CM)
+        actb[:, 8 : 8 + H, :] = silu(half).reshape(8, H, CM)
         for r in range(8):
             rows, at = (rc_even, k * 4 + r // 2) if r % 2 == 0 else (rc_odd, k * 4 + r // 2 + 1)
             for b in range(3):
@@ -199,6 +204,17 @@
     for copy, sends, _ in forward:
         pl.when(sends)(copy.start)
 
+    for copy in weights[1:]:
+        copy.wait()
+    wback[...] = jnp.zeros_like(wback)
+
+    def tap(a, b):
+        return ws[a, b * CM : (b + 1) * CM, :]
+
+    for slot, a in ((0, 1), (1, 2), (2, 0)):
+        wback[slot, 0:CM, 0:CM] = tap(a, 1)
+        wback[slot, CM : 2 * CM, 0:CM] = tap(a, 2)
+        wback[slot, CM : 2 * CM, CM : 2 * CM] = tap(a, 0)
     def even_rows(m):
         x = img[2 * m].astype(F32)
         for half in range(2):
@@ -206,15 +222,15 @@
         for half in range(2):
             evp[m, :, half * CM : (half + 1) * CM] = evb[half, pl.ds(0, Q, stride=2), :].astype(BF16)
 
-    loop(Q, even_rows)
+    loop(Q // 4, lambda m: unrolled(4, lambda i: even_rows(4 * m + i)))
 
     def project(b):
         at = pl.ds(b * 8 * Q, 8 * Q)
         p = dot(evp[pl.ds(b * 8, 8)].reshape(8 * Q, CI), wp[...])
         npj[at, :] = p
-        r_p[at, :] = lax.rsqrt(lane_mean(sum(p[:, lanes(k)] * p[:, lanes(k)] for k in range(4)), ones_o) + EPSILON)
-
-    loop(6, project)
+        r_p[at, :] = half_scale(sum(p[:, lanes(k)] * p[:, lanes(k)] for k in range(4)), ones_o)
+
+    loop(3, lambda b: unrolled(2, lambda i: project(2 * b + i)))
 
     for copy, sends, takes in forward:
         pl.when(takes)(copy.wait_recv)
@@ -249,28 +265,30 @@
         def convolve(b):
             at = i0 + b * 8
             v = sum(dot(taps(a, at, 8), ws[a]) for a in range(3))
-            psp[pl.ds(b * 8 * Q, 8 * Q), :] = v
-            spat[pl.ds(b * 8 * Q, 8 * Q), :] = act(v, ones_m).astype(BF16)
-
-        loop(2, convolve)
+            scale = half_scale(v * v, ones_m)
+            half = v * scale
+            psp[0, pl.ds(b * 8 * Q, 8 * Q), :] = half
+            psp[1, pl.ds(b * 8 * Q, 8 * Q), :] = scale
+            spat[pl.ds(b * 8 * Q, 8 * Q), :] = silu(half).astype(BF16)
+
+        unrolled(2, convolve)
 
         def expand(b):
             at = pl.ds(b * 8 * Q, 8 * Q)
             e = dot(spat[at, :], we[...])
             ne[at, :] = e
-            r_e[at, :] = lax.rsqrt(lane_mean(sum(e[:, lanes(k)] * e[:, lanes(k)] for k in range(4)), ones_o) + EPSILON)
-
-        loop(2, expand)
+            r_e[at, :] = half_scale(sum(e[:, lanes(k)] * e[:, lanes(k)] for k in range(4)), ones_o)
+
+        unrolled(2, expand)
         feat[...] = jnp.zeros_like(feat)
 
         def merge(b):
             at = pl.ds(b * 4 * Q, 4 * Q)
             out = pl.ds(i0 * Q + b * 4 * Q, 4 * Q)
-            h_e, h_p = 0.5 * r_e[at, :], 0.5 * r_p[out, :]
+            h_e, h_p = r_e[at, :], r_p[out, :]
             for k in range(4):
                 half = ne[at, lanes(k)] * h_e + npj[out, lanes(k)] * h_p
-                merged = half * jnp.tanh(half) + half
-                feat[:, lanes(k)] += jnp.sum(merged.reshape(4, Q, CM), axis=0)
+                feat[:, lanes(k)] += jnp.sum(silu(half).reshape(4, Q, CM), axis=0)
 
         loop(4, merge)
 
@@ -294,8 +312,7 @@
             z_e, z_p = 0.0, 0.0
             for k in range(4):
                 n_e, n_p = ne[at, lanes(k)] * s_e, npj[out, lanes(k)] * s_p
-                slope = silu_slope(0.5 * (n_e + n_p)).reshape(4, Q, CM)
-                dn = (slope * gb[:, lanes(k)][None]).reshape(4 * Q, CM)
+                dn = silu_vjp((n_e + n_p).reshape(4, Q, CM), gb[:, lanes(k)][None]).reshape(4 * Q, CM)
                 dnb[:, lanes(k)] = dn
                 z_e, z_p = z_e + dn * n_e, z_p + dn * n_p
             m_e, m_p = lane_mean(z_e, ones_o), lane_mean(z_p, ones_o)
@@ -313,7 +330,7 @@
         def unconvolve(b):
             at = pl.ds(b * 8 * Q, 8 * Q)
             g = dot_nt(eg[at, :], we[...])
-            d = act_vjp(psp[at, :], g, ones_m)
+            d = act_vjp(psp[0, at, :], psp[1, at, :], g, ones_m)
             dbuf[:, 0:Q, :] = d.reshape(8, Q, CM)
             d16 = d.astype(BF16)
             dcat[pl.ds(i0 + b * 8, 8), :, 0:CM] = d16.reshape(8, Q, CM)
@@ -321,7 +338,7 @@
                 dcat[i0 + b * 8 + r, :, CM : 2 * CM] = dbuf[r, 1 : Q + 1, :].astype(BF16)
                 dcol[pl.ds(i0 + b * 8 + r, 1), :] = dbuf[r, 0:1, :]
 
-        loop(2, unconvolve)
+        unrolled(2, unconvolve)
 
     loop(3, tile_row)
 
@@ -365,9 +382,23 @@
     def piece(p):
         return pl.ds(pl.multiple_of(p * PIECE, PIECE), PIECE)
 
+    core, cy = lax.rem(col, 2), col // 2
+    half_rows = NC // 2 * CHUNK
+
+    def core_half(c):
+        return pl.ds(pl.multiple_of(c * half_rows, half_rows), half_rows)
+
+    def y_chunk(y):
+        return chunk(core * (NC // 2) + y)
+
+    other = {"col": col + 1 - 2 * core}
+
+    def scatter0(d):
+        return remote(s1.at[core_half(1 - core)], r0, sem0.at[0], sem0.at[1], other)
+
     def scatter1(d):
-        peer = lax.rem(col + d, NC)
-        return remote(s1.at[chunk(peer)], r1.at[col], sem1.at[0, d], sem1.at[1, d], {"col": peer})
+        peer = lax.rem(cy + d, NC // 2)
+        return remote(s1.at[y_chunk(peer)], r1.at[cy], sem1.at[0, d], sem1.at[1, d], {"col": 2 * peer + core})
 
     def scatter2(d):
         q = lax.rem(grp + d, ng)
@@ -377,7 +408,11 @@
         return remote(a3.at[piece(grp)], a3.at[piece(grp)], sem3.at[0, d], sem3.at[1, d], grp_peer(d))
 
     def gather4(d):
-        return remote(s3, r4.at[col], sem4.at[0, d], sem4.at[1, d], col_peer(d))
+        peer = lax.rem(cy + d, NC // 2)
+        return remote(s3, r4.at[y_chunk(cy)], sem4.at[0, d], sem4.at[1, d], {"col": 2 * peer + core})
+
+    def gather8(d):
+        return remote(r4.at[core_half(core)], r4.at[core_half(core)], sem8.at[0], sem8.at[1], other)
 
     def scatter5(d):
         peer = lax.rem(col + d, NC)
@@ -389,7 +424,16 @@
     def gather7(d):
         return remote(a7, r7.at[col], sem7.at[0, d], sem7.at[1, d], col_peer(d))
 
-    start(NC - 1, scatter1)
+    start(1, scatter0)
+
+    finish(1, scatter0)
+
+    def add_core(y):
+        mine = y_chunk(y)
+        s1[mine, :] = (s1[mine, :].astype(F32) + r0[chunk(y), :].astype(F32)).astype(BF16)
+
+    loop(NC // 2, add_core)
+    start(NC // 2 - 1, scatter1)
 
     for copy, sends, takes in backward:
         pl.when(takes)(copy.wait_recv)
@@ -417,24 +461,27 @@
             for rp in range(2):
                 at = 2 * (i0 + 4 * c)
                 for cp in range(2):
-                    v = jnp.concatenate([pre[at + 2 * i + rp, pl.ds(cp, Q, stride=2), :] for i in range(4)], axis=0)
+                    half, scale = (
+                        jnp.concatenate([ref[at + 2 * i + rp, pl.ds(cp, Q, stride=2), :] for i in range(4)], axis=0)
+                        for ref in (pre, prs)
+                    )
                     g = eo[rp, pl.ds(4 * c, 4), :, lanes(cp)].reshape(4 * Q, CM)
-                    d = act_vjp(v, g, ones_m)
+                    d = act_vjp(half, scale, g, ones_m)
                     for i in range(4):
                         natb[rp, i, pl.ds(cp, Q, stride=2), :] = d[i * Q : (i + 1) * Q]
                 for i in range(4):
                     prg16[at + 2 * i + rp] = natb[rp, i].astype(BF16)
 
-        loop(2, some_rows)
+        unrolled(2, some_rows)
         rows = pl.ds(2 * i0, 16)
         a_wr[...] += dot_tn(prg16[rows].reshape(16 * H, CM), img[rows].reshape(16 * H, CI))
 
-    loop(6, pass3)
-
-    finish(NC - 1, scatter1)
-    r1[col] = s1[chunk(col), :]
-    a1[...] = sum(r1[p].astype(F32) for p in range(NC))
+    loop(3, pass3)
+    finish(NC // 2 - 1, scatter1)
+    r1[cy] = s1[y_chunk(cy), :]
+    a1[...] = sum(r1[p].astype(F32) for p in range(NC // 2))
     start(ng - 1, scatter2)
+    loop(3, lambda b: pass3(b + 3))
 
     for p in range(NC):
         s5[p, 32:40, :] = jnp.zeros((8, CM), F32)
@@ -445,10 +492,6 @@
         for p in range(4):
             s5[half * 4 + p, 0:32, :] = t[p * 32 : (p + 1) * 32, :]
     start(NC - 1, scatter5)
-
-    def image_out(k):
-        rows = pl.ds(k * 8, 8)
-        return pltpu.make_async_copy(img.at[rows], gimg_hbm.at[0, rows], sem_out.at[k])
 
     def pass4(k):
         main = dot_nt(prg16[pl.ds(k * 8, 8)].reshape(8 * H, CM), wr[...])
@@ -464,34 +507,37 @@
     def some(lo, hi):
         loop(hi - lo, lambda k: pass4(lo + k))
 
-    some(0, 4)
     finish(ng - 1, scatter2)
     r2[grp] = a1[piece(grp), :]
     a3[piece(grp), :] = sum(r2[p] for p in range(ng)) * SCALE
     start(ng - 1, gather3)
+    some(0, 4)
     finish(NC - 1, scatter5)
     r5[col] = s5[col]
     a5[...] = sum(r5[p] for p in range(NC))
     r6[grp] = a5[...]
     start(ng - 1, gather6)
-    some(4, 8)
+    some(4, 6)
     finish(ng - 1, gather3)
     s3[...] = a3[...].astype(BF16)
-    r4[col] = s3[...]
-    start(NC - 1, gather4)
+    r4[y_chunk(cy), :] = s3[...]
+    start(NC // 2 - 1, gather4)
+    some(6, 9)
     finish(ng - 1, gather6)
     a7[...] = sum(r6[p] for p in range(ng))
     r7[col] = a7[...]
     start(NC - 1, gather7)
-    some(8, 12)
-    finish(NC - 1, gather4)
+    some(9, 12)
+    finish(NC // 2 - 1, gather4)
+    start(1, gather8)
     finish(NC - 1, gather7)
+    finish(1, gather8)
 
     for p in range(3):
-        o_spatial[p * CHUNK : (p + 1) * CHUNK, :] = r4[p].astype(F32)
+        o_spatial[p * CHUNK : (p + 1) * CHUNK, :] = r4[p * CHUNK : (p + 1) * CHUNK, :].astype(F32)
 
     def summed(at, n):
-        return r4[at // CHUNK, at % CHUNK : at % CHUNK + n, :].astype(F32)
+        return r4[at : at + n, :].astype(F32)
 
     for q in range(4):
         o_expand[:, q * CM : (q + 1) * CM] = summed(1152 + q * 128, 128)
@@ -521,7 +567,12 @@
     v = pltpu.VMEM
     dma = pltpu.SemaphoreType.DMA
     scratch = [
+        v((CI, CM), BF16),
+        v((3, 3 * CM, CM), BF16),
+        v((CM, CO), BF16),
+        v((CI, CO), BF16),
         v((H, H, CI), BF16),
+        v((H, H, CM), F32),
         v((H, H, CM), F32),
         v((8, 8 + H, CM), F32),
         v((Q + 1, Q, 3 * CM), BF16),
@@ -534,7 +585,7 @@
         v((16, CM), BF16),
         v((H + 16, CM), F32),
         v((Q, 3 * CM), BF16),
-        v((TB * Q, CM), F32),
+        v((2, TB * Q, CM), F32),
         v((TB * Q, CM), BF16),
         v((TB * Q, CO), F32),
         v((Q * Q, CO), F32),
@@ -563,12 +614,13 @@
         v((CM, CI), F32),
         v((8, CM), F32),
         v((NC * CHUNK, CM), BF16),
-        v((NC, CHUNK, CM), BF16),
+        v((NC // 2 * CHUNK, CM), BF16),
+        v((NC // 2, CHUNK, CM), BF16),
         v((CHUNK, CM), F32),
         v((NR * NS, PIECE, CM), F32),
         v((CHUNK, CM), F32),
         v((CHUNK, CM), BF16),
-        v((NC, CHUNK, CM), BF16),
+        v((NC * CHUNK, CM), BF16),
         v((NC, 40, CM), F32),
         v((NC, 40, CM), F32),
         v((40, CM), F32),
@@ -576,9 +628,10 @@
         v((40, CM), F32),
         v((NC, 40, CM), F32),
         dma((IMG_CHUNKS,)),
-        dma((12,)),
+        dma((4,)),
         dma((6,)),
         dma((6,)),
+        dma((2,)),
         dma((2, NC)),
         dma((2, NR * NS)),
         dma((2, NR * NS)),
@@ -586,12 +639,13 @@
         dma((2, NC)),
         dma((2, NR * NS)),
         dma((2, NC)),
+        dma((2,)),
     ]
     shapes = [image.shape, (CI, CM), (9 * CM, CM), (CM, CO), (CI, CO), (2, CO), (1, 1)]
     out = pl.pallas_call(
         kernel,
         out_shape=[v(s, BF16 if k == 0 else F32) for k, s in enumerate(shapes)],
-        in_specs=[hbm] + [vmem] * 6 + [pl.BlockSpec(memory_space=pltpu.SMEM)],
+        in_specs=[hbm] * 5 + [vmem] * 2 + [pl.BlockSpec(memory_space=pltpu.SMEM)],
         out_specs=[vmem] * 7,
         scratch_shapes=scratch,
         compiler_params=pltpu.CompilerParams(

time: 77.2 us -> 65.8 us (0.85)
  Pallas kernels: 75.7 us -> 64.4 us
    pallas_call x1, Pallas kernels: 72.4 us -> 61 us  [per_device(): pl.pallas_call(kernel, out_shape=[v(s, BF16 if k == 0 else F32) for k, s...]
where the time goes in v3:
time: 65.8 us; the launch traced here: 65.6 us
  Pallas kernels  64.4 us (98%)
  between operations  1.29 us (2%)
    pallas_call x1, Pallas kernels, per_device(): pl.pallas_call(kernel, out_shape=[v(s, BF16 if k == 0 else F32) for k, s...  61 us
    pallas_call x1, Pallas kernels, per_device(): pl.pallas_call(hand_over, out_shape=[jax.ShapeDtypeStruct(o.shape, o.dtyp...  3.34 us

profile of v3, /device:TPU:1, one launch (start us, length us, event | category | flops | bytes accessed | tf_op | source)
XLA Modules:
  0.0 65.6 jit_solution(17413788335882976598)
XLA Ops:
  1.3 61.0 %shard_map.135 = (bf16[1,96,96,256]{3,2,1,0:T(8,128)(2,1)S(1)}, f32[256,128]{1,0:T(8,128)S(1)}, f32[1152,128]{1,0:T(8,128)S(1)}, f32[128,512]{1,0:T(8,128)S(1)},...) custom-call(bf16[1,96,96,256]{3,2,1,0:T(8,128)(2,1)} %img_hbm.1, bf16[256,128]{1,0:T(8,128)(2,1)} %wr_hbm.1, ...), custom_call_target="tpu_custom_call" | custom-call | flops 7000000000 | bytes 12000000 | tf_op jit(solution)/shard_map/pallas_call | solution.py:645
  62.3 3.3 %shard_map.136 = (bf16[1,96,96,256]{3,2,1,0:T(8,128)(2,1)}, f32[256,128]{1,0:T(8,128)}, f32[1152,128]{1,0:T(8,128)}, f32[128,512]{1,0:T(8,128)}, f32[256,512]{1,...) custom-call(bf16[1,96,96,256]{3,2,1,0:T(8,128)(2,1)S(1)} %get-tuple-element.21.refs_0_, ...), custom_call_target="tpu_custom_call" | custom-call | tf_op jit(solution)/shard_map/pallas_call | solution.py:656

commit v4 on v3

--- a/solution.py
+++ b/solution.py
@@ -128,11 +128,6 @@
     dbuf[:, Q : Q + 8, :] = jnp.zeros_like(dbuf[:, Q : Q + 8, :])
     ones_m = jnp.full((CM, CM), 4.0 / CM, BF16)
     ones_o = jnp.full((CM, CM), 4.0 / CO, BF16)
-    a_ws[...] = jnp.zeros_like(a_ws)
-    a_we[...] = jnp.zeros_like(a_we)
-    a_wp[...] = jnp.zeros_like(a_wp)
-    a_wr[...] = jnp.zeros_like(a_wr)
-    a_misc[...] = jnp.zeros_like(a_misc)
 
     @pl.when(jnp.logical_not(has_up))
     def _():
@@ -204,6 +199,11 @@
     for copy, sends, _ in forward:
         pl.when(sends)(copy.start)
 
+    a_ws[...] = jnp.zeros_like(a_ws)
+    a_we[...] = jnp.zeros_like(a_we)
+    a_wp[...] = jnp.zeros_like(a_wp)
+    a_wr[...] = jnp.zeros_like(a_wr)
+    a_misc[...] = jnp.zeros_like(a_misc)
     for copy in weights[1:]:
         copy.wait()
     wback[...] = jnp.zeros_like(wback)
@@ -250,7 +250,71 @@
         patch_left(rc_even, m, hcolf[pl.ds(2 * m, 1), :])
         patch_left(rc_odd, m + 1, hcolf[pl.ds(2 * m + 1, 1), :])
 
-    loop(Q, patch_rows)
+    loop(Q // 4, lambda m: unrolled(4, lambda i: patch_rows(4 * m + i)))
+
+    ng = NR * NS
+
+    def start(n, make):
+        loop(n, lambda d: make(d + 1).start())
+
+    def finish(n, make):
+        loop(n, lambda d: make(d + 1).wait())
+
+    def chunk(p):
+        return pl.ds(pl.multiple_of(p * CHUNK, CHUNK), CHUNK)
+
+    def piece(p):
+        return pl.ds(pl.multiple_of(p * PIECE, PIECE), PIECE)
+
+    core, cy = lax.rem(col, 2), col // 2
+    half_rows = NC // 2 * CHUNK
+
+    def y_chunk(y):
+        return chunk(core * (NC // 2) + y)
+
+    other = {"col": col + 1 - 2 * core}
+
+    def scatter0(part):
+        size = half_rows // 2
+        src = s1.at[pl.ds(pl.multiple_of((1 - core) * half_rows + part * size, size), size)]
+        return remote(src, r0.at[pl.ds(part * size, size)], sem0.at[0, part], sem0.at[1, part], other)
+
+    def add_part(part):
+        scatter0(part).wait()
+        for y in (2 * part, 2 * part + 1):
+            mine = y_chunk(y)
+            s1[mine, :] = (s1[mine, :].astype(F32) + r0[y * CHUNK : (y + 1) * CHUNK, :].astype(F32)).astype(BF16)
+        for d in range(1, NC // 2):
+            pl.when(lax.rem(cy + d, NC // 2) // 2 == part)(scatter1(d).start)
+
+    def scatter1(d):
+        peer = lax.rem(cy + d, NC // 2)
+        return remote(s1.at[y_chunk(peer)], r1.at[cy], sem1.at[0, d], sem1.at[1, d], {"col": 2 * peer + core})
+
+    def scatter2(d):
+        q = lax.rem(grp + d, ng)
+        return remote(a1.at[piece(q)], r2.at[grp], sem2.at[0, d], sem2.at[1, d], grp_peer(d))
+
+    def gather3(d):
+        return remote(a3.at[piece(grp)], a3.at[piece(grp)], sem3.at[0, d], sem3.at[1, d], grp_peer(d))
+
+    def gather4(d):
+        peer = lax.rem(cy + d, NC // 2)
+        return remote(s3, r4.at[y_chunk(cy)], sem4.at[0, d], sem4.at[1, d], {"col": 2 * peer + core})
+
+    def gather8(d):
+        there = r4.at[y_chunk(lax.rem(cy - d + NC // 2, NC // 2))]
+        return remote(there, there, sem8.at[0, d], sem8.at[1, d], other)
+
+    def scatter5(d):
+        peer = lax.rem(col + d, NC)
+        return remote(s5.at[peer], r5.at[col], sem5.at[0, d], sem5.at[1, d], {"col": peer})
+
+    def gather6(d):
+        return remote(a5, r6.at[grp], sem6.at[0, d], sem6.at[1, d], grp_peer(d))
+
+    def gather7(d):
+        return remote(a7, r7.at[col], sem7.at[0, d], sem7.at[1, d], col_peer(d))
 
     npx = TB * Q
 
@@ -258,6 +322,11 @@
         if a == 1:
             return rc_even[pl.ds(at, n)].reshape(n * Q, 3 * CM)
         return rc_odd[pl.ds(at + a // 2, n)].reshape(n * Q, 3 * CM)
+
+    def spatial_weight_grad(u):
+        d16 = dcat[pl.ds(u * TB, TB), :, 0:CM].reshape(npx, CM)
+        for a in range(3):
+            a_ws[:, a * 3 * CM : (a + 1) * 3 * CM] += dot_tn(d16, taps(a, u * TB, TB))
 
     def tile_row(u):
         i0 = u * TB
@@ -327,6 +396,9 @@
         a_we[...] += dot_tn(spat[...], eg[...])
         a_wp[...] += dot_tn(evp[pl.ds(i0, TB)].reshape(npx, CI), pg[pl.ds(i0 * Q, npx), :])
 
+    def back_row(u):
+        i0 = u * TB
+
         def unconvolve(b):
             at = pl.ds(b * 8 * Q, 8 * Q)
             g = dot_nt(eg[at, :], we[...])
@@ -340,7 +412,30 @@
 
         unrolled(2, unconvolve)
 
-    loop(3, tile_row)
+    def both(u):
+        tile_row(u)
+        back_row(u)
+        spatial_weight_grad(u)
+
+    e_slot, s_slot = (0, 1, 4, 5), (2, 3, 6)
+
+    def e_rows(r):
+        at = e_slot[r // CHUNK] * CHUNK + r % CHUNK
+        return slice(at, at + CM)
+
+    def s_rows(t):
+        at = s_slot[t // 3] * CHUNK + t % 3 * CM
+        return slice(at, at + CM)
+
+    loop(2, both)
+    tile_row(2)
+    for q in range(4):
+        s1[e_rows(q * CM), :] = a_we[:, lanes(q)].astype(BF16)
+        for part in range(2):
+            s1[e_rows(512 + (2 * q + part) * CM), :] = a_wp[part * CM : (part + 1) * CM, lanes(q)].astype(BF16)
+    s1[7 * CHUNK :, :] = jnp.zeros((CHUNK, CM), BF16)
+    scatter0(0).start()
+    back_row(2)
 
     drow[...] = dcat[0]
     col16[0:Q] = dcol[...].astype(BF16)
@@ -354,87 +449,12 @@
     for copy, sends, _ in backward:
         pl.when(sends)(copy.start)
 
-    def spatial_weight_grad(u):
-        d16 = dcat[pl.ds(u * TB, TB), :, 0:CM].reshape(npx, CM)
-        for a in range(3):
-            a_ws[:, a * 3 * CM : (a + 1) * 3 * CM] += dot_tn(d16, taps(a, u * TB, TB))
-
-    loop(3, spatial_weight_grad)
-
+    add_part(0)
+    spatial_weight_grad(2)
     for t in range(9):
-        s1[t * CM : (t + 1) * CM, :] = a_ws[:, t * CM : (t + 1) * CM].T.astype(BF16)
-    for q in range(4):
-        s1[1152 + q * 128 : 1152 + (q + 1) * 128, :] = a_we[:, q * CM : (q + 1) * CM].astype(BF16)
-        s1[1664 + q * 256 : 1664 + (q + 1) * 256, :] = a_wp[:, q * CM : (q + 1) * CM].astype(BF16)
-    s1[2688:3072, :] = jnp.zeros((384, CM), BF16)
-
-    ng = NR * NS
-
-    def start(n, make):
-        loop(n, lambda d: make(d + 1).start())
-
-    def finish(n, make):
-        loop(n, lambda d: make(d + 1).wait())
-
-    def chunk(p):
-        return pl.ds(pl.multiple_of(p * CHUNK, CHUNK), CHUNK)
-
-    def piece(p):
-        return pl.ds(pl.multiple_of(p * PIECE, PIECE), PIECE)
-
-    core, cy = lax.rem(col, 2), col // 2
-    half_rows = NC // 2 * CHUNK
-
-    def core_half(c):
-        return pl.ds(pl.multiple_of(c * half_rows, half_rows), half_rows)
-
-    def y_chunk(y):
-        return chunk(core * (NC // 2) + y)
-
-    other = {"col": col + 1 - 2 * core}
-
-    def scatter0(d):
-        return remote(s1.at[core_half(1 - core)], r0, sem0.at[0], sem0.at[1], other)
-
-    def scatter1(d):
-        peer = lax.rem(cy + d, NC // 2)
-        return remote(s1.at[y_chunk(peer)], r1.at[cy], sem1.at[0, d], sem1.at[1, d], {"col": 2 * peer + core})
-
-    def scatter2(d):
-        q = lax.rem(grp + d, ng)
-        return remote(a1.at[piece(q)], r2.at[grp], sem2.at[0, d], sem2.at[1, d], grp_peer(d))
-
-    def gather3(d):
-        return remote(a3.at[piece(grp)], a3.at[piece(grp)], sem3.at[0, d], sem3.at[1, d], grp_peer(d))
-
-    def gather4(d):
-        peer = lax.rem(cy + d, NC // 2)
-        return remote(s3, r4.at[y_chunk(cy)], sem4.at[0, d], sem4.at[1, d], {"col": 2 * peer + core})
-
-    def gather8(d):
-        return remote(r4.at[core_half(core)], r4.at[core_half(core)], sem8.at[0], sem8.at[1], other)
-
-    def scatter5(d):
-        peer = lax.rem(col + d, NC)
-        return remote(s5.at[peer], r5.at[col], sem5.at[0, d], sem5.at[1, d], {"col": peer})
-
-    def gather6(d):
-        return remote(a5, r6.at[grp], sem6.at[0, d], sem6.at[1, d], grp_peer(d))
-
-    def gather7(d):
-        return remote(a7, r7.at[col], sem7.at[0, d], sem7.at[1, d], col_peer(d))
-
-    start(1, scatter0)
-
-    finish(1, scatter0)
-
-    def add_core(y):
-        mine = y_chunk(y)
-        s1[mine, :] = (s1[mine, :].astype(F32) + r0[chunk(y), :].astype(F32)).astype(BF16)
-
-    loop(NC // 2, add_core)
-    start(NC // 2 - 1, scatter1)
-
+        s1[s_rows(t), :] = a_ws[:, lanes(t)].T.astype(BF16)
+    scatter0(1).start()
+    add_part(1)
     for copy, sends, takes in backward:
         pl.when(takes)(copy.wait_recv)
         pl.when(sends)(copy.wait_send)
@@ -522,27 +542,28 @@
     s3[...] = a3[...].astype(BF16)
     r4[y_chunk(cy), :] = s3[...]
     start(NC // 2 - 1, gather4)
+    gather8(0).start()
     some(6, 9)
     finish(ng - 1, gather6)
     a7[...] = sum(r6[p] for p in range(ng))
     r7[col] = a7[...]
     start(NC - 1, gather7)
     some(9, 12)
-    finish(NC // 2 - 1, gather4)
-    start(1, gather8)
+    for d in range(1, NC // 2):
+        gather4(d).wait_recv()
+        gather8(d).start()
     finish(NC - 1, gather7)
-    finish(1, gather8)
-
-    for p in range(3):
-        o_spatial[p * CHUNK : (p + 1) * CHUNK, :] = r4[p * CHUNK : (p + 1) * CHUNK, :].astype(F32)
-
-    def summed(at, n):
-        return r4[at : at + n, :].astype(F32)
-
+    for d in range(1, NC // 2):
+        gather4(d).wait_send()
+    for d in range(NC // 2):
+        gather8(d).wait()
+
+    for t in range(9):
+        o_spatial[t * CM : (t + 1) * CM, :] = r4[s_rows(t), :].astype(F32)
     for q in range(4):
-        o_expand[:, q * CM : (q + 1) * CM] = summed(1152 + q * 128, 128)
+        o_expand[:, lanes(q)] = r4[e_rows(q * CM), :].astype(F32)
         for part in range(2):
-            o_project[part * 128 : (part + 1) * 128, q * CM : (q + 1) * CM] = summed(1664 + q * 256 + part * 128, 128)
+            o_project[part * CM : (part + 1) * CM, lanes(q)] = r4[e_rows(512 + (2 * q + part) * CM), :].astype(F32)
     for p in range(NC):
         o_reduce[p * 32 : (p + 1) * 32, :] = r7[p, 0:32, :]
     for k in range(4):
@@ -631,7 +652,7 @@
         dma((4,)),
         dma((6,)),
         dma((6,)),
-        dma((2,)),
+        dma((2, 2)),
         dma((2, NC)),
         dma((2, NR * NS)),
         dma((2, NR * NS)),
@@ -639,7 +660,7 @@
         dma((2, NC)),
         dma((2, NR * NS)),
         dma((2, NC)),
-        dma((2,)),
+        dma((2, NC)),
     ]
     shapes = [image.shape, (CI, CM), (9 * CM, CM), (CM, CO), (CI, CO), (2, CO), (1, 1)]
     out = pl.pallas_call(

time: 65.8 us -> 64 us (0.973)
  Pallas kernels: 64.4 us -> 62.4 us
    pallas_call x1, Pallas kernels: 61 us -> 59.1 us  [per_device(): pl.pallas_call(kernel, out_shape=[v(s, BF16 if k == 0 else F32) for k, s...]
where the time goes in v4:
time: 64 us; the launch traced here: 63.7 us
  Pallas kernels  62.4 us (98%)
  between operations  1.29 us (2%)
    pallas_call x1, Pallas kernels, per_device(): pl.pallas_call(kernel, out_shape=[v(s, BF16 if k == 0 else F32) for k, s...  59.1 us
    pallas_call x1, Pallas kernels, per_device(): pl.pallas_call(hand_over, out_shape=[jax.ShapeDtypeStruct(o.shape, o.dtyp...  3.34 us

profile of v4, /device:TPU:1, one launch (start us, length us, event | category | flops | bytes accessed | tf_op | source)
XLA Modules:
  0.0 63.7 jit_solution(662505741005022448)
XLA Ops:
  1.3 59.1 %shard_map.135 = (bf16[1,96,96,256]{3,2,1,0:T(8,128)(2,1)S(1)}, f32[256,128]{1,0:T(8,128)S(1)}, f32[1152,128]{1,0:T(8,128)S(1)}, f32[128,512]{1,0:T(8,128)S(1)},...) custom-call(bf16[1,96,96,256]{3,2,1,0:T(8,128)(2,1)} %img_hbm.1, bf16[256,128]{1,0:T(8,128)(2,1)} %wr_hbm.1, ...), custom_call_target="tpu_custom_call" | custom-call | flops 7000000000 | bytes 12000000 | tf_op jit(solution)/shard_map/pallas_call | solution.py:666
  60.4 3.3 %shard_map.136 = (bf16[1,96,96,256]{3,2,1,0:T(8,128)(2,1)}, f32[256,128]{1,0:T(8,128)}, f32[1152,128]{1,0:T(8,128)}, f32[128,512]{1,0:T(8,128)}, f32[256,512]{1,...) custom-call(bf16[1,96,96,256]{3,2,1,0:T(8,128)(2,1)S(1)} %get-tuple-element.21.refs_0_, ...), custom_call_target="tpu_custom_call" | custom-call | tf_op jit(solution)/shard_map/pallas_call | solution.py:677

commit v5 on v4

--- a/solution.py
+++ b/solution.py
@@ -166,7 +166,13 @@
         image_copy(k).wait()
         x = img[pl.ds(k * 8, 8)].reshape(8 * H, CI)
         v = dot(x, wr[...])
-        scale = half_scale(v * v, ones_m)
+        cut = 192
+        by_lane = lax.rsqrt(
+            jnp.sum(v[:cut] * v[:cut], axis=-1, keepdims=True) * (4.0 / CM) + 4.0 * EPSILON
+        )
+        scale = jnp.concatenate(
+            [jnp.broadcast_to(by_lane, (cut, CM)), half_scale(v[cut:] * v[cut:], ones_m)], axis=0
+        )
         half = v * scale
         pre[pl.ds(k * 8, 8)] = half.reshape(8, H, CM)
         prs[pl.ds(k * 8, 8)] = scale.reshape(8, H, CM)
@@ -230,7 +236,7 @@
         npj[at, :] = p
         r_p[at, :] = half_scale(sum(p[:, lanes(k)] * p[:, lanes(k)] for k in range(4)), ones_o)
 
-    loop(3, lambda b: unrolled(2, lambda i: project(2 * b + i)))
+    loop(2, lambda b: unrolled(3, lambda i: project(3 * b + i)))
 
     for copy, sends, takes in forward:
         pl.when(takes)(copy.wait_recv)
@@ -511,7 +517,6 @@
         t = a_wr[:, lanes(half)].T * SCALE
         for p in range(4):
             s5[half * 4 + p, 0:32, :] = t[p * 32 : (p + 1) * 32, :]
-    start(NC - 1, scatter5)
 
     def pass4(k):
         main = dot_nt(prg16[pl.ds(k * 8, 8)].reshape(8 * H, CM), wr[...])
@@ -531,6 +536,7 @@
     r2[grp] = a1[piece(grp), :]
     a3[piece(grp), :] = sum(r2[p] for p in range(ng)) * SCALE
     start(ng - 1, gather3)
+    start(NC - 1, scatter5)
     some(0, 4)
     finish(NC - 1, scatter5)
     r5[col] = s5[col]

time: 64 us -> 66.2 us (1.034)
  Pallas kernels: 62.4 us -> 64.7 us
    pallas_call x1, Pallas kernels: 59.1 us -> 61.4 us  [per_device(): pl.pallas_call(kernel, out_shape=[v(s, BF16 if k == 0 else F32) for k, s...]
where the time goes in v5:
time: 66.2 us; the launch traced here: 66 us
  Pallas kernels  64.7 us (98%)
  between operations  1.29 us (2%)
    pallas_call x1, Pallas kernels, per_device(): pl.pallas_call(kernel, out_shape=[v(s, BF16 if k == 0 else F32) for k, s...  61.4 us
    pallas_call x1, Pallas kernels, per_device(): pl.pallas_call(hand_over, out_shape=[jax.ShapeDtypeStruct(o.shape, o.dtyp...  3.34 us

profile of v5, /device:TPU:1, one launch (start us, length us, event | category | flops | bytes accessed | tf_op | source)
XLA Modules:
  0.0 66.0 jit_solution(15354718951366711790)
XLA Ops:
  1.3 61.4 %shard_map.135 = (bf16[1,96,96,256]{3,2,1,0:T(8,128)(2,1)S(1)}, f32[256,128]{1,0:T(8,128)S(1)}, f32[1152,128]{1,0:T(8,128)S(1)}, f32[128,512]{1,0:T(8,128)S(1)},...) custom-call(bf16[1,96,96,256]{3,2,1,0:T(8,128)(2,1)} %img_hbm.1, bf16[256,128]{1,0:T(8,128)(2,1)} %wr_hbm.1, ...), custom_call_target="tpu_custom_call" | custom-call | flops 7000000000 | bytes 12000000 | tf_op jit(solution)/shard_map/pallas_call | solution.py:672
  62.7 3.3 %shard_map.136 = (bf16[1,96,96,256]{3,2,1,0:T(8,128)(2,1)}, f32[256,128]{1,0:T(8,128)}, f32[1152,128]{1,0:T(8,128)}, f32[128,512]{1,0:T(8,128)}, f32[256,512]{1,...) custom-call(bf16[1,96,96,256]{3,2,1,0:T(8,128)(2,1)S(1)} %get-tuple-element.21.refs_0_, ...), custom_call_target="tpu_custom_call" | custom-call | tf_op jit(solution)/shard_map/pallas_call | solution.py:683
